TPU v7x, 32 devices: a whole 2x2x4 slice. The times are simulated.
32 devices in a mesh: seq: 4 (over z), dp: 8 (over y, x, core).
Axes of the slice: x: 2, y: 2, z: 4, core: 2. Of those that a mesh axis runs over, the one named last changes fastest.
Arguments:
- layer_input: bfloat16 [8192, 1024], P(('dp', 'seq')), may hold values from -6 to 6
- out_grad: bfloat16 [8192, 1024], P(('dp', 'seq')), may hold values from -6 to 6
- lengths: int32 [8, 3], P('dp'), may hold values from 1 to 682, 1024 in all within a row
- item_owner: int32 [8192, 1], P(('dp', 'seq')), may hold values from 0 to 31; in each aligned block of 256 rows (0 to 255, 256 to 511, ...) at most 16 rows name the same one
- item_row: int32 [8192], P(('dp', 'seq')), may hold values from 0 to 511
- w_attn: bfloat16 [1024, 3072], replicated, may hold values from -0.1875 to 0.1875
- w_gate: bfloat16 [1024, 1024], replicated, may hold values from -0.1875 to 0.1875
- w_out: bfloat16 [1024, 1024], replicated, may hold values from -0.1875 to 0.1875
- emb_table: float32 [16384, 1024], P(('seq', 'dp')), may hold values from -6 to 6
- row_accum: float32 [16384], P(('seq', 'dp')), may hold values from 0.25 to 4
Outputs:
- grad_attn: float32 [1024, 3072], P('dp', 'seq')
- grad_gate: float32 [1024, 1024], P('dp', 'seq')
- grad_out: float32 [1024, 1024], P('dp', 'seq')
- new_table: float32 [16384, 1024], P(('seq', 'dp'))
- new_accum: float32 [16384], P(('seq', 'dp'))
Inputs may be any that keep to these rules, and one draw needn't show every extreme that they name: Each group's 3 lengths sum to 1024; the largest is exactly 682. `item_owner`: among the 256 events of one device at most 16 name one owner, a bound that some block reaches.
All inputs are finite; a program needn't handle non-finite values.
Results may differ from a plain program's by a relative error of at most 0.0092.
Values may be sent and summed in bfloat16 or wider, within the bound.
No kernel may reach another device: no remote copies, remote signals or barrier semaphores. Data moves between devices by JAX's collectives and lax.ppermute only.
A program may use at most 128 MiB of HBM per device.

v0:
```python
import functools

import jax
import jax.numpy as jnp
from jax import lax
from jax.experimental import pallas as pl
from jax.experimental.pallas import tpu as pltpu
from jax.sharding import PartitionSpec as P

D = 1024
H = 16
DH = 64
PAIR = 2 * DH

NORM_EPS = 1e-05
LEARN_RATE = 0.1
VMEM_LIMIT = 56 * 1024 * 1024
BF = jnp.bfloat16
F32 = jnp.float32


def dot_nn(a, b):
    return lax.dot_general(a, b, (((1,), (0,)), ((), ())), preferred_element_type=F32)


def dot_nt(a, b):
    return lax.dot_general(a, b, (((1,), (1,)), ((), ())), preferred_element_type=F32)


def history_start(lengths_ref, users, place):
    start = jnp.zeros_like(place)
    end = jnp.int32(0)
    for user in range(users - 1):
        end = end + lengths_ref[0, user]
        start = jnp.where(place >= end, end, start)
    return start


def head_columns(kind, head):
    first = head * 3 * DH + kind * DH
    return slice(first, first + DH)


def split_pairs(acts_ref, split_ref, kind, block, blk):
    at = pl.ds(pl.multiple_of(block * blk, blk), blk)
    zero = jnp.zeros((blk, DH), BF)
    for p in range(split_ref.shape[0]):
        one, two = (acts_ref[at, head_columns(kind, 2 * p + h)] for h in range(2))
        below = pl.multiple_of(block * 2 * blk + blk, blk)
        split_ref[p, pl.ds(pl.multiple_of(block * 2 * blk, blk), blk), :] = jnp.concatenate([one, zero], axis=1)
        split_ref[p, pl.ds(below, blk), :] = jnp.concatenate([zero, two], axis=1)


def forward_kernel(*refs, blk, users, maxlen, count):
    lengths_ref, order_ref = refs[:2]
    x_refs = refs[2 : 2 + count]
    w_ref = refs[2 + count]
    outs = refs[3 + count :]
    if count > 1:
        x_out_ref, outs = outs[0], outs[1:]
    acts_ref, slopes_ref, gate_ref, weights_ref, score_slope_ref, heads_ref, k_t, v_split = outs
    i = pl.program_id(0)
    heads = weights_ref.shape[0]
    attn = 3 * heads * DH
    chunks = x_refs[0].shape[0] // blk

    @pl.when(i == 0)
    def _():
        for b in range(count):
            for r in range(chunks):
                at = pl.ds(pl.multiple_of(order_ref[b * chunks + r] * blk, blk), blk)
                x = x_refs[b][r * blk : (r + 1) * blk, :]
                if count > 1:
                    x_out_ref[at, :] = x
                for lane in range(0, w_ref.shape[1], 512):
                    lanes = slice(lane, lane + 512)
                    half = 0.5 * dot_nn(x, w_ref[:, lanes])
                    t = jnp.tanh(half)
                    prod = half * t
                    silu = half + prod
                    acts_ref[at, lanes] = silu.astype(BF)
                    slopes_ref[at, lanes] = (0.5 * (1.0 + t) * (1.0 + half - prod)).astype(BF)
                    skip = max(0, attn - lane)
                    if skip < 512:
                        gate_ref[at, lane + skip - attn : lane + 512 - attn] = silu[:, skip:]
                for h in range(heads):
                    k_t[h * DH : (h + 1) * DH, at] = jnp.transpose(acts_ref[at, head_columns(2, h)])
                split_pairs(acts_ref, v_split, 0, order_ref[b * chunks + r], blk)

    at_i = pl.ds(pl.multiple_of(i * blk, blk), blk)
    q_half = [acts_ref[at_i, head_columns(1, h)] * jnp.asarray(0.5 * DH**-0.5, BF) for h in range(heads)]
    row = i * blk + lax.broadcasted_iota(jnp.int32, (blk, blk), 0)
    col0 = lax.broadcasted_iota(jnp.int32, (blk, blk), 1)
    start = history_start(lengths_ref, users, row)

    def column(j, acc):
        at_j = pl.ds(pl.multiple_of(j * blk, blk), blk)
        both_j = pl.ds(pl.multiple_of(j * 2 * blk, 2 * blk), 2 * blk)
        col = col0 + j * blk
        allowed = (col <= row) & (col >= start)
        per_head = []
        for h in range(heads):
            half = dot_nn(q_half[h], k_t[h * DH : (h + 1) * DH, at_j])
            half = jnp.where(allowed, half, -64.0)
            t = jnp.tanh(half)
            p = half * t
            weights = (half + p).astype(BF)
            weights_ref[h, :, at_j] = weights
            score_slope_ref[h, :, at_j] = ((1.0 + t) * (1.0 + half - p)).astype(BF)
            per_head.append(weights)
        return tuple(
            acc[p] + dot_nn(jnp.concatenate(per_head[2 * p : 2 * p + 2], axis=1), v_split[p, both_j, :])
            for p in range(heads // 2)
        )

    first = history_start(lengths_ref, users, i * blk) // blk
    zero = jnp.zeros((blk, PAIR), F32)
    acc = lax.fori_loop(first, i + 1, column, (zero,) * (heads // 2))
    heads_ref[...] = (jnp.concatenate(acc, axis=1) * (1.0 / maxlen)).astype(BF)


def forward_attention(lengths, order, x_blocks, w_own, blk, maxlen):
    count = len(x_blocks)
    block_rows = x_blocks[0].shape[0]
    positions = count * block_rows
    cols = w_own.shape[1] // 4
    heads = cols // DH
    users = lengths.shape[1]
    elements = heads * positions * positions // 2
    whole = lambda i: (0, 0)
    out_specs = [
        pl.BlockSpec((positions, 4 * cols), whole),
        pl.BlockSpec((positions, 4 * cols), whole),
        pl.BlockSpec((positions, cols), whole),
        pl.BlockSpec((heads, blk, positions), lambda i: (0, i, 0)),
        pl.BlockSpec((heads, blk, positions), lambda i: (0, i, 0)),
        pl.BlockSpec((blk, cols), lambda i: (i, 0)),
    ]
    out_shape = [
        jax.ShapeDtypeStruct((positions, 4 * cols), BF),
        jax.ShapeDtypeStruct((positions, 4 * cols), BF),
        jax.ShapeDtypeStruct((positions, cols), F32),
        jax.ShapeDtypeStruct((heads, positions, positions), BF),
        jax.ShapeDtypeStruct((heads, positions, positions), BF),
        jax.ShapeDtypeStruct((positions, cols), BF),
    ]
    if count > 1:
        out_specs = [pl.BlockSpec((positions, D), whole)] + out_specs
        out_shape = [jax.ShapeDtypeStruct((positions, D), BF)] + out_shape
    return pl.pallas_call(
        functools.partial(forward_kernel, blk=blk, users=users, maxlen=maxlen, count=count),
        grid=(positions // blk,),
        in_specs=[pl.BlockSpec(memory_space=pltpu.SMEM), pl.BlockSpec(memory_space=pltpu.SMEM)]
        + [pl.BlockSpec((block_rows, D), whole)] * count
        + [pl.BlockSpec((D, 4 * cols), whole)],
        out_specs=out_specs,
        out_shape=out_shape,
        scratch_shapes=[pltpu.VMEM((cols, positions), BF), pltpu.VMEM((cols // PAIR, 2 * positions, PAIR), BF)],
        compiler_params=pltpu.CompilerParams(vmem_limit_bytes=VMEM_LIMIT),
        cost_estimate=pl.CostEstimate(
            flops=8 * positions * D * cols + 4 * elements * 256,
            bytes_accessed=4 * positions * D + 4 * elements,
            transcendentals=elements,
        ),
        name="attention_forward",
    )(lengths, order, *x_blocks, w_own)


def stats_kernel(*refs, blk, count):
    order_ref = refs[0]
    og_refs = refs[1 : 1 + count]
    w_ref, gate_ref, heads_ref = refs[1 + count : 4 + count]
    outs = refs[4 + count :]
    if count > 1:
        og_out_ref, outs = outs[0], outs[1:]
    mg_ref, stats_ref = outs
    chunks = og_refs[0].shape[0] // blk
    for b in range(count):
        for r in range(chunks):
            at = pl.ds(pl.multiple_of(order_ref[b * chunks + r] * blk, blk), blk)
            og = og_refs[b][r * blk : (r + 1) * blk, :]
            if count > 1:
                og_out_ref[at, :] = og
            mg = dot_nt(og, w_ref[...])
            mg_ref[at, :] = mg
            ng = mg * gate_ref[at, :]
            heads = heads_ref[at, :].astype(F32)
            mean = jnp.mean(heads, axis=1, keepdims=True)
            centred = heads - mean
            square = jnp.sum(centred * centred, axis=1, keepdims=True)
            total = jnp.sum(ng, axis=1, keepdims=True)
            cross = jnp.sum(ng * centred, axis=1, keepdims=True)
            lane = lax.broadcasted_iota(jnp.int32, (blk, 128), 1)
            packed = jnp.where(lane == 0, mean, jnp.where(lane == 1, square, jnp.where(lane == 2, total, cross)))
            stats_ref[:, at] = jnp.transpose(packed)[:8, :]


def event_stats(order, og_blocks, w_out_own, gate, heads, blk):
    positions, cols = heads.shape
    count = len(og_blocks)
    vmem = pl.BlockSpec(memory_space=pltpu.VMEM)
    out_shape = [
        jax.ShapeDtypeStruct((positions, cols), F32),
        jax.ShapeDtypeStruct((8, positions), F32),
    ]
    if count > 1:
        out_shape = [jax.ShapeDtypeStruct((positions, D), BF)] + out_shape
    return pl.pallas_call(
        functools.partial(stats_kernel, blk=blk, count=count),
        in_specs=[pl.BlockSpec(memory_space=pltpu.SMEM)] + [vmem] * (count + 3),
        out_specs=[vmem] * len(out_shape),
        out_shape=out_shape,
        compiler_params=pltpu.CompilerParams(vmem_limit_bytes=VMEM_LIMIT),
        cost_estimate=pl.CostEstimate(
            flops=2 * positions * cols * D, bytes_accessed=4 * positions * D + 10 * positions * cols, transcendentals=0
        ),
        name="event_stats",
    )(order, *og_blocks, w_out_own, gate, heads)


def combined_stats(stats_refs, cols):
    shards = len(stats_refs)
    positions = stats_refs[0].shape[1]
    means = [ref[0:1, :] for ref in stats_refs]
    mean = sum(means) * (1.0 / shards)
    square = jnp.zeros_like(mean)
    total = jnp.zeros_like(mean)
    cross = jnp.zeros_like(mean)
    for s, ref in enumerate(stats_refs):
        shift = means[s] - mean
        part = ref[2:3, :]
        square = square + ref[1:2, :] + cols * shift * shift
        total = total + part
        cross = cross + ref[3:4, :] + shift * part
    inv_dev = lax.rsqrt(square * (1.0 / D) + NORM_EPS)
    kind = lax.broadcasted_iota(jnp.int32, (128, positions), 0)
    rest = jnp.where(kind == 2, total * (1.0 / D), cross * inv_dev * (1.0 / D))
    packed = jnp.where(kind == 0, mean, jnp.where(kind == 1, inv_dev, rest))
    per_event = jnp.transpose(packed)
    return [per_event[:, k : k + 1] for k in range(4)]


def backward_kernel(*refs, blk, users, maxlen, shards):
    lengths_ref = refs[0]
    stats_refs = refs[1 : 1 + shards]
    mg_ref, gate_ref, heads_ref, acts_ref, slopes_ref, weights_ref, score_slope_ref = refs[1 + shards : 8 + shards]
    grad_ref, mixed_ref, o_ref, o_t, q_t, v_t, k_split, vg_t, kg_t, qg = refs[8 + shards :]
    i = pl.program_id(0)
    positions, cols = o_ref.shape
    heads = cols // DH
    blocks = positions // blk
    scale = DH ** (-0.5)

    @pl.when(i == 0)
    def _():
        mean, inv_dev, total, cross = combined_stats(stats_refs, cols)
        for p in range(heads // 2):
            lanes = slice(p * PAIR, (p + 1) * PAIR)
            normed = (heads_ref[:, lanes].astype(F32) - mean) * inv_dev
            gate = gate_ref[:, lanes]
            mg = mg_ref[:, lanes]
            mixed_ref[:, lanes] = (normed * gate).astype(BF)
            gate_lanes = slice(3 * cols + p * PAIR, 3 * cols + (p + 1) * PAIR)
            gate_slope = slopes_ref[:, gate_lanes].astype(F32)
            grad_ref[:, gate_lanes] = (mg * normed * gate_slope).astype(BF)
            o_ref[:, lanes] = (inv_dev * (mg * gate - total - normed * cross)).astype(BF)
        o_t[...] = jnp.transpose(o_ref[...])
        for scratch, kind in ((v_t, 0), (q_t, 1)):
            scratch[...] = jnp.transpose(jnp.concatenate([acts_ref[:, head_columns(kind, h)] for h in range(heads)], axis=1))
        for block in range(blocks):
            split_pairs(acts_ref, k_split, 2, block, blk)
        vg_t[...] = jnp.zeros_like(vg_t)
        kg_t[...] = jnp.zeros_like(kg_t)

    at_i = pl.ds(pl.multiple_of(i * blk, blk), blk)
    o_i = [o_ref[at_i, h * DH : (h + 1) * DH] for h in range(heads)]

    def column(j, acc):
        at_j = pl.ds(pl.multiple_of(j * blk, blk), blk)
        both_j = pl.ds(pl.multiple_of(j * 2 * blk, 2 * blk), 2 * blk)
        per_head = []
        for h in range(heads):
            lanes = slice(h * DH, (h + 1) * DH)
            weight_grad = dot_nn(o_i[h], v_t[lanes, at_j])
            score_grad = (weight_grad * score_slope_ref[h, :, at_j].astype(F32)).astype(BF)
            vg_t[lanes, at_j] += dot_nn(o_t[lanes, at_i], weights_ref[h, :, at_j])
            kg_t[lanes, at_j] += dot_nn(q_t[lanes, at_i], score_grad)
            per_head.append(score_grad)
        return tuple(
            acc[p] + dot_nn(jnp.concatenate(per_head[2 * p : 2 * p + 2], axis=1), k_split[p, both_j, :])
            for p in range(heads // 2)
        )

    first = history_start(lengths_ref, users, i * blk) // blk
    zero = jnp.zeros((blk, PAIR), F32)
    acc = lax.fori_loop(first, i + 1, column, (zero,) * (heads // 2))
    qg[at_i, :] = jnp.concatenate(acc, axis=1)

    @pl.when(i == blocks - 1)
    def _():
        factor = 0.5 * scale / maxlen
        grads = [jnp.transpose(vg_t[...]) * (1.0 / maxlen), qg[...] * factor, jnp.transpose(kg_t[...]) * factor]
        pieces = [grads[kind][:, h * DH : (h + 1) * DH] for h in range(heads) for kind in range(3)]
        for n in range(3 * heads // 2):
            lanes = slice(n * PAIR, (n + 1) * PAIR)
            grad = jnp.concatenate(pieces[2 * n : 2 * n + 2], axis=1).astype(BF).astype(F32)
            grad_ref[:, lanes] = (grad * slopes_ref[:, lanes].astype(F32)).astype(BF)


def backward_attention(lengths, stats, mg, gate, head_outs, acts, slopes, weights, score_slope, blk, maxlen):
    positions, cols = mg.shape
    heads = cols // DH
    shards = len(stats)
    users = lengths.shape[1]
    elements = heads * positions * positions // 2
    whole = lambda i: (0, 0)
    return pl.pallas_call(
        functools.partial(backward_kernel, blk=blk, users=users, maxlen=maxlen, shards=shards),
        grid=(positions // blk,),
        in_specs=[pl.BlockSpec(memory_space=pltpu.SMEM)]
        + [pl.BlockSpec((8, positions), whole)] * shards
        + [
            pl.BlockSpec((positions, cols), whole),
            pl.BlockSpec((positions, cols), whole),
            pl.BlockSpec((positions, cols), whole),
            pl.BlockSpec((positions, 4 * cols), whole),
            pl.BlockSpec((positions, 4 * cols), whole),
            pl.BlockSpec((heads, blk, positions), lambda i: (0, i, 0)),
            pl.BlockSpec((heads, blk, positions), lambda i: (0, i, 0)),
        ],
        out_specs=[pl.BlockSpec((positions, 4 * cols), whole), pl.BlockSpec((positions, cols), whole)],
        out_shape=[
            jax.ShapeDtypeStruct((positions, 4 * cols), BF),
            jax.ShapeDtypeStruct((positions, cols), BF),
        ],
        scratch_shapes=[
            pltpu.VMEM((positions, cols), BF),
            pltpu.VMEM((cols, positions), BF),
            pltpu.VMEM((cols, positions), BF),
            pltpu.VMEM((cols, positions), BF),
            pltpu.VMEM((cols // PAIR, 2 * positions, PAIR), BF),
            pltpu.VMEM((cols, positions), F32),
            pltpu.VMEM((cols, positions), F32),
            pltpu.VMEM((positions, cols), F32),
        ],
        compiler_params=pltpu.CompilerParams(vmem_limit_bytes=VMEM_LIMIT),
        cost_estimate=pl.CostEstimate(
            flops=8 * elements * 256, bytes_accessed=4 * elements + 26 * positions * cols, transcendentals=0
        ),
        name="attention_backward",
    )(lengths, *stats, mg, gate, head_outs, acts, slopes, weights, score_slope)


def update_kernel(rows_ref, table_ref, accum_ref, new_table_ref, new_accum_ref, ids):
    i = pl.program_id(0)
    blk = table_ref.shape[0]
    slots = rows_ref.shape[0]

    @pl.when(i == 0)
    def _():
        numbers = jnp.transpose(rows_ref[:, D:].astype(F32))
        ids[...] = (numbers[0:1, :] * 256.0 + numbers[1:2, :]).astype(jnp.int32)

    row = i * blk + lax.broadcasted_iota(jnp.int32, (blk, slots), 0)
    hits = jnp.where(row == ids[...], 1.0, 0.0).astype(BF)
    grad = dot_nn(hits, rows_ref[:, :D])
    accum = jnp.transpose(jnp.broadcast_to(accum_ref[...], (128, blk)))[:, :1] + jnp.mean(grad * grad, axis=1, keepdims=True)
    new_accum_ref[...] = jnp.transpose(jnp.broadcast_to(accum, (blk, 128)))[:1, :]
    new_table_ref[...] = table_ref[...] - LEARN_RATE * grad * lax.rsqrt(accum)


def update_rows(got_rows, emb_table, row_accum):
    rows_own = emb_table.shape[0]
    slots = got_rows.shape[0]
    blk = min(256, rows_own)
    new_table, new_accum = pl.pallas_call(
        update_kernel,
        grid=(rows_own // blk,),
        in_specs=[
            pl.BlockSpec((slots, D + 128), lambda i: (0, 0)),
            pl.BlockSpec((blk, D), lambda i: (i, 0)),
            pl.BlockSpec((1, blk), lambda i: (0, i)),
        ],
        out_specs=[
            pl.BlockSpec((blk, D), lambda i: (i, 0)),
            pl.BlockSpec((1, blk), lambda i: (0, i)),
        ],
        out_shape=[
            jax.ShapeDtypeStruct((rows_own, D), F32),
            jax.ShapeDtypeStruct((1, rows_own), F32),
        ],
        scratch_shapes=[pltpu.VMEM((1, slots), jnp.int32)],
        compiler_params=pltpu.CompilerParams(vmem_limit_bytes=VMEM_LIMIT),
        cost_estimate=pl.CostEstimate(
            flops=2 * rows_own * slots * D, bytes_accessed=8 * rows_own * D + 2 * slots * D, transcendentals=rows_own
        ),
        name="update_rows",
    )(got_rows, emb_table, row_accum.reshape(1, rows_own))
    return new_table, new_accum.reshape(rows_own)


def own_weights(w_attn, w_gate, part, cols):
    attn = lax.dynamic_slice_in_dim(w_attn, part * 3 * cols, 3 * cols, 1)
    gate = lax.dynamic_slice_in_dim(w_gate, part * cols, cols, 1)
    return jnp.concatenate([attn, gate], axis=1)


def row_slots(owners, rows, devices, capacity):
    events = owners.shape[0]
    owner_hits = (owners[:, None] == jnp.arange(devices, dtype=jnp.int32)[None, :]).astype(BF)
    place = jnp.arange(events, dtype=jnp.int32)
    before = (place[:, None] > place[None, :]).astype(BF)
    earlier = jnp.dot(before, owner_hits, preferred_element_type=F32)
    slots = jnp.sum(earlier * owner_hits.astype(F32), axis=1).astype(jnp.int32)
    flat_slot = owners * capacity + slots
    slot_hits = jnp.arange(devices * capacity, dtype=jnp.int32)[:, None] == flat_slot[None, :]
    lane = jnp.arange(128, dtype=jnp.int32)[None, :]
    numbers = jnp.where(lane == 0, rows[:, None] // 256, jnp.where(lane == 1, rows[:, None] % 256, 0))
    return slot_hits.astype(BF), numbers.astype(BF)


def to_owners(rows, devices, capacity):
    shape = (devices, capacity) + rows.shape[1:]
    got = lax.all_to_all(rows.reshape(shape), ("seq", "dp"), split_axis=0, concat_axis=0, tiled=True)
    return got.reshape(rows.shape)


TN = (((0,), (0,)), ((), ()))


def dot_tn(a, b):
    return lax.dot_general(a, b, TN, preferred_element_type=F32)


def body_whole(
    layer_input, out_grad, lengths, item_owner, item_row, w_attn, w_gate, w_out, emb_table, row_accum
):
    seq_count = lax.axis_size("seq")
    dp_count = lax.axis_size("dp")
    devices = seq_count * dp_count
    seq_id = lax.axis_index("seq")
    tokens_dev = layer_input.shape[0]
    positions = tokens_dev * seq_count
    maxlen = 2 * positions // 3
    blk = min(256, positions)
    cols = D // seq_count
    capacity = max(2, 2 * tokens_dev // devices)

    w_own = own_weights(w_attn, w_gate, seq_id, cols)
    w_out_own = lax.dynamic_slice_in_dim(w_out, seq_id * cols, cols, 0)
    slot_matrix, numbers = row_slots(item_owner[:, 0], item_row, devices, capacity)

    x_full = lax.all_gather(layer_input, "seq", axis=0, tiled=True)
    og_full = lax.all_gather(out_grad, "seq", axis=0, tiled=True)
    order = jnp.arange(positions // blk, dtype=jnp.int32)
    acts, slopes, gate, weights, score_slope, heads = forward_attention(
        lengths, order, [x_full], w_own, blk, maxlen
    )
    mg, stats_own = event_stats(order, [og_full], w_out_own, gate, heads, blk)
    stats = lax.all_gather(stats_own, "seq", axis=0, tiled=False)
    grads, mixed = backward_attention(
        lengths, [stats[s] for s in range(seq_count)], mg, gate, heads, acts, slopes, weights, score_slope, blk, maxlen
    )

    input_part = dot_nt(grads, w_own).astype(BF)
    got = lax.all_to_all(
        input_part.reshape(seq_count, tokens_dev, D), "seq", split_axis=0, concat_axis=0, tiled=True
    )
    input_grad = jnp.sum(got.astype(F32), axis=0) + out_grad.astype(F32)
    rows = jnp.concatenate([input_grad.astype(BF), numbers], axis=1)
    rows = jnp.dot(slot_matrix, rows, preferred_element_type=F32).astype(BF)
    got_rows = to_owners(rows, devices, capacity)
    new_table, new_accum = update_rows(got_rows, emb_table, row_accum)

    out_part = dot_tn(mixed, og_full).astype(BF)
    share = dp_count // seq_count
    out_part = out_part.reshape(share, D // dp_count, seq_count, cols).transpose(0, 2, 1, 3).reshape(D, cols)
    merged = jnp.concatenate([dot_tn(x_full, grads).astype(BF), out_part], axis=1)
    merged = lax.psum_scatter(merged, "dp", scatter_dimension=0, tiled=True)
    steps = []
    for s in range(seq_count):
        for piece in range(dp_count):
            part, target = divmod(piece, seq_count)
            steps.append((s * dp_count + piece, target * dp_count + s * share + part))
    grad_out = lax.ppermute(merged[:, 4 * cols :], ("seq", "dp"), steps).astype(F32)
    grad_attn = merged[:, : 3 * cols].astype(F32)
    grad_gate = merged[:, 3 * cols : 4 * cols].astype(F32)
    return (grad_attn, grad_gate, grad_out, new_table, new_accum)


SEQ = 4
PLANE = 4


def send(array, target):
    steps = []
    for s in range(SEQ):
        for e in range(PLANE):
            for c in range(2):
                to = target(s, e, c)
                if to is not None:
                    steps.append((s * 2 * PLANE + 2 * e + c, to[0] * 2 * PLANE + 2 * to[1] + to[2]))
    return lax.ppermute(array, ("seq", "dp"), steps)


def home(s, c):
    return c == s // 2


def swap_far(array):
    return send(array, lambda s, e, c: None if home(s, c) else (3 - s, e, 1 - c))


def fetch_near(array):
    return send(array, lambda s, e, c: (s ^ 1, e, c) if home(s, c) else ((3 - s) ^ 1, e, 1 - c))


def swap_near(array):
    return send(array, lambda s, e, c: (s ^ 1, e, c))


def swap_core(array):
    return send(array, lambda s, e, c: (s, e, 1 - c))


def swap_x(array):
    return send(array, lambda s, e, c: (s, e ^ 1, c))


def swap_y(array):
    return send(array, lambda s, e, c: (s, e ^ 2, c))


def tie(*arrays):
    return lax.optimization_barrier(arrays)


def sums_kernel(proj_one, proj_two, out_one, out_two, attn_ref, gate_ref, out_ref):
    cut = attn_ref.shape[1]
    attn_ref[...] = proj_one[:, :cut].astype(F32) + proj_two[:, :cut].astype(F32)
    gate_ref[...] = proj_one[:, cut:].astype(F32) + proj_two[:, cut:].astype(F32)
    out_ref[...] = out_one[...].astype(F32) + out_two[...].astype(F32)


def last_sums(proj, out):
    rows, cols = out[0].shape
    widths = (proj[0].shape[1] - cols, cols, cols)
    return pl.pallas_call(
        sums_kernel,
        in_specs=[pl.BlockSpec(memory_space=pltpu.VMEM)] * 4,
        out_specs=[pl.BlockSpec(memory_space=pltpu.VMEM)] * 3,
        out_shape=[jax.ShapeDtypeStruct((rows, width), F32) for width in widths],
        compiler_params=pltpu.CompilerParams(vmem_limit_bytes=VMEM_LIMIT),
        cost_estimate=pl.CostEstimate(flops=0, bytes_accessed=12 * rows * cols * 5, transcendentals=0),
        name="last_sums",
    )(*proj, *out)


def halves(array, bit, axis):
    kept = lax.dynamic_index_in_dim(array, bit, axis, keepdims=False)
    sent = lax.dynamic_index_in_dim(array, 1 - bit, axis, keepdims=False)
    return kept, sent


def body_pairs(
    layer_input, out_grad, lengths, item_owner, item_row, w_attn, w_gate, w_out, emb_table, row_accum
):
    devices = 2 * PLANE * SEQ
    s = lax.axis_index("seq")
    d = lax.axis_index("dp")
    e, c = d // 2, d % 2
    y, x = e // 2, e % 2
    tokens_dev = layer_input.shape[0]
    positions = tokens_dev * SEQ
    maxlen = 2 * positions // 3
    blk = min(256, positions)
    cols = D // SEQ
    rows_own = emb_table.shape[0]
    capacity = max(2, 2 * tokens_dev // devices)
    at_home = c == s // 2
    part = 2 * (s % 2) + c

    def block_of(seq, core):
        return jnp.where(core == seq // 2, seq, 3 - seq)

    mine_at, near_at = block_of(s, c), block_of(s ^ 1, c)
    core_at, diag_at = block_of(s, 1 - c), block_of(s ^ 1, 1 - c)
    order = jnp.stack([mine_at, near_at, core_at, diag_at]).astype(jnp.int32)

    x_far = swap_far(layer_input)
    x_near = fetch_near(layer_input)
    users = lengths.shape[1]
    keys = (item_owner[:, 0] * rows_own + item_row).reshape(1, tokens_dev)
    small = jnp.concatenate([keys, jnp.pad(lengths, ((0, 0), (0, 128 - users)))], axis=1)
    small = jnp.where(at_home, small, swap_far(small))
    keys, lengths = small[0, :tokens_dev], small[:, tokens_dev : tokens_dev + users]
    w_own = own_weights(w_attn, w_gate, part, cols)
    w_out_own = lax.dynamic_slice_in_dim(w_out, part * cols, cols, 0)
    slot_matrix, numbers = row_slots(keys // rows_own, keys % rows_own, devices, capacity)
    x_far, x_near, w_own, w_out_own, slot_matrix, numbers, lengths = tie(
        x_far, x_near, w_own, w_out_own, slot_matrix, numbers, lengths
    )
    x_here = jnp.concatenate([jnp.where(at_home, layer_input, x_far), x_near], axis=0)
    x_there = swap_core(x_here)
    x_here, og_own = tie(x_here, out_grad)
    og_near = fetch_near(og_own)
    og_far = swap_far(og_own)

    x_full, acts, slopes, gate, weights, score_slope, heads = forward_attention(
        lengths, order, [x_here, x_there], w_own, blk, maxlen
    )
    og_far, og_near, heads = tie(og_far, og_near, heads)
    og_mine = jnp.where(at_home, og_own, og_far)
    og_here = jnp.concatenate([og_mine, og_near], axis=0)
    og_there = swap_core(og_here)
    og_full, mg, stats_own = event_stats(order, [og_here, og_there], w_out_own, gate, heads, blk)
    stats = [
        stats_own,
        swap_core(stats_own),
        swap_near(stats_own),
        send(stats_own, lambda s, e, c: (s ^ 1, e, 1 - c)),
    ]
    grads, mixed = backward_attention(
        lengths, stats, mg, gate, heads, acts, slopes, weights, score_slope, blk, maxlen
    )

    def input_part(grads, block):
        return dot_nt(lax.dynamic_slice_in_dim(grads, block * tokens_dev, tokens_dev, 0), w_own)

    from_diag = swap_core(input_part(grads, diag_at).astype(BF))
    near_sum = (input_part(grads, near_at) + from_diag.astype(F32)).astype(BF)
    near_sum, grads = tie(near_sum, grads)
    from_near = swap_near(near_sum)
    core_part = input_part(grads, core_at).astype(BF)
    from_core = swap_core(core_part)
    input_grad = input_part(grads, mine_at) + og_mine.astype(F32)

    core_part, grads, mixed = tie(core_part, grads, mixed)
    half = 5 * cols // 2
    proj = dot_tn(x_full, grads).astype(BF).reshape(2, 2, D // PLANE, 4 * cols)
    out_part = dot_tn(mixed, og_full).astype(BF).reshape(cols, 2, 2, cols)
    a_kept, a_sent = halves(proj[..., :half], x, 1)
    b_kept, b_sent = halves(proj[..., half:], y, 0)
    out_kept, out_sent = (piece.transpose(1, 0, 2) for piece in halves(out_part, y, 1))
    b_kept = jnp.concatenate([b_kept, out_kept], axis=-1)
    b_sent = jnp.concatenate([b_sent, out_sent], axis=-1)
    a_got = swap_x(a_sent)
    b_got = swap_y(b_sent)

    input_grad = input_grad + from_core.astype(F32) + from_near.astype(F32)
    rows = jnp.concatenate([input_grad.astype(BF), numbers], axis=1)
    rows = jnp.dot(slot_matrix, rows, preferred_element_type=F32).astype(BF)
    rows, a_got, b_got = tie(rows, a_got, b_got)
    got_rows = to_owners(rows, devices, capacity)

    a = (a_kept.astype(F32) + a_got.astype(F32)).astype(BF)
    b = (b_kept.astype(F32) + b_got.astype(F32)).astype(BF)
    a_kept, a_sent = halves(a, y, 0)
    b_kept, b_sent = halves(b, x, 0)
    a = (a_kept.astype(F32) + swap_y(a_sent).astype(F32)).astype(BF)
    b = (b_kept.astype(F32) + swap_x(b_sent).astype(F32)).astype(BF)

    def last(array, target):
        pieces = array.reshape(2, D // (2 * PLANE), array.shape[1])
        one, other = halves(pieces, s // 2, 0)
        one = send(one, lambda s, e, c: target(s, e, c, s // 2))
        return one, send(other, lambda s, e, c: target(s, e, c, 1 - s // 2))

    proj = jnp.concatenate([a, b[:, : 4 * cols - half]], axis=1)
    proj = last(proj, lambda s, e, c, piece: (2 * (s % 2) + c, e, piece))
    out = last(b[:, 4 * cols - half :], lambda s, e, c, piece: (e, 2 * (s % 2) + c, piece))
    new_table, new_accum = update_rows(got_rows, emb_table, row_accum)
    *proj, new_accum = tie(*proj, new_accum)
    attn, gate, grad_out = last_sums(proj, out)
    return (attn, gate, grad_out, new_table, new_accum)


def solution(mesh):
    placed = (
        P(("dp", "seq"), None),
        P(("dp", "seq"), None),
        P("dp", None),
        P(("dp", "seq"), None),
        P(("dp", "seq")),
        P(),
        P(),
        P(),
        P(("seq", "dp"), None),
        P(("seq", "dp")),
    )
    paired = mesh.shape["seq"] == SEQ and mesh.shape["dp"] == 2 * PLANE
    return jax.shard_map(
        body_pairs if paired else body_whole,
        mesh=mesh,
        in_specs=placed,
        out_specs=(
            P("dp", "seq"),
            P("dp", "seq"),
            P("dp", "seq"),
            P(("seq", "dp"), None),
            P(("seq", "dp")),
        ),
        check_vma=False,
    )
```

profile of v0, /device:TPU:0, one launch (start us, length us, event | category | flops | bytes accessed | tf_op | source)
XLA Modules:
  0.0 180.7 jit_solution(12335351445400888249)
XLA Ops:
  1.5 3.1 %collective-permute-start.1 = (bf16[256,1024]{1,0:T(8,128)(2,1)}, bf16[256,1024]{1,0:T(8,128)(2,1)}, u32[]{:S(2)}, u32[]{:S(2)}) collective-permute-start(bf16[256,1024]{1,0:T(8,128)(2,1)} %param.10), channel_id=1, source_target_pairs={{0,8},{1,16},{2,10},{3,18},{4,12},{5,20},{6,14},{7,22},{8,0},{9,24... | collective-permute-start | bytes 1572872 | tf_op jit(solution)/shard_map/ppermute | solution.py:503
  7.4 1.9 %constant_dynamic-slice_fusion.2.refs_3_ = bf16[256,1024]{1,0:T(8,128)(2,1)} fusion(bf16[1024,1024]{1,0:T(8,128)(2,1)} %param.17, s32[]{:T(128)S(6)} %select_n.173), kind=kLoop, calls=%fused_computation.58 | loop fusion | bytes 1048580 | tf_op jit(solution)/shard_map/dynamic_slice | solution.py:598
  10.8 1.6 pad_maximum_fusion.refs_4_
  15.7 16.4 %collective-permute-start.3 = (bf16[512,1024]{1,0:T(8,128)(2,1)S(1)}, bf16[512,1024]{1,0:T(8,128)(2,1)}, u32[]{:S(2)}, u32[]{:S(2)}) collective-permute-start(bf16[512,1024]{1,0:T(8,128)(2,1)S(1)} %pad_maximum_fusion.1.refs_2_), channel_id=1, source_target_pairs={{0,1},{1,0},{2,3},{3,2},{4,5},{5,4},{6,7},{7,6},{8,9},{9,8},{10,11... | collective-permute-start | bytes 3145736 | tf_op jit(solution)/shard_map/ppermute | solution.py:503
  32.8 2.3 %collective-permute-start.5 = (bf16[256,1024]{1,0:T(8,128)(2,1)S(1)}, bf16[256,1024]{1,0:T(8,128)(2,1)S(1)}, u32[]{:S(2)}, u32[]{:S(2)}) collective-permute-start(bf16[256,1024]{1,0:T(8,128)(2,1)S(1)} %copy-done.11), channel_id=1, source_target_pairs={{0,8},{1,16},{2,10},{3,18},{4,12},{5,20},{6,14},{7,22},{8,0},{9,24... | collective-permute-start | bytes 1572872 | tf_op jit(solution)/shard_map/ppermute | solution.py:503
  35.7 16.8 %attention_forward.1 = (bf16[1024,1024]{1,0:T(8,128)(2,1)}, bf16[1024,1024]{1,0:T(8,128)(2,1)}, bf16[1024,1024]{1,0:T(8,128)(2,1)}, f32[1024,256]{1,0:T(8,128)},...) custom-call(s32[1,3]{1,0:T(1,128)} %slice.25.refs_0_, ...), custom_call_target="tpu_custom_call" | custom-call | flops 4294967296 | bytes 12582912 | tf_op jit(solution)/shard_map/attention_forward/pallas_call | solution.py:150
  52.7 8.7 %collective-permute-start.6 = (bf16[512,1024]{1,0:T(8,128)(2,1)S(1)}, bf16[512,1024]{1,0:T(8,128)(2,1)S(1)}, u32[]{:S(2)}, u32[]{:S(2)}) collective-permute-start(bf16[512,1024]{1,0:T(8,128)(2,1)S(1)} %pad_maximum_fusion.2.refs_1_), channel_id=1, source_target_pairs={{0,1},{1,0},{2,3},{3,2},{4,5},{5,4},{6,7},{7,6},{8,9},{9,8},{10,11... | collective-permute-start | bytes 3145736 | tf_op jit(solution)/shard_map/ppermute | solution.py:503
  61.4 2.3 %collective-permute-done.6.refs_2_ = bf16[512,1024]{1,0:T(8,128)(2,1)S(1)} collective-permute-done((bf16[512,1024]{1,0:T(8,128)(2,1)S(1)}, bf16[512,1024]{1,0:T(8,128)(2,1)S(1)}, u32[]{:S(2)}, u32[]{:S(2)}) %collective-permute-start.6) | collective-permute-done | bytes 1048608 | tf_op jit(solution)/shard_map/ppermute | solution.py:503
  64.7 4.6 %event_stats.1 = (bf16[1024,1024]{1,0:T(8,128)(2,1)}, f32[1024,256]{1,0:T(8,128)}, f32[8,1024]{1,0:T(8,128)}) custom-call(s32[4]{0:T(128)} %pad_add_fusion.1.refs_1_.refs_0_, bf16[512,1024]{1,0:T(8,128)(2,1)} %copy-done.3, bf16[512,1024]{1,0:T(8,128)(2,1)} %copy-done.7, bf16[256,1024]{1,0:T(8,128)(2,1)} %constant_dynamic-slice_fusion.2.refs_3_, ...), custom_call_target="tpu_custom_call" | custom-call | flops 536870912 | bytes 6815744 | tf_op jit(solution)/shard_map/event_stats/pallas_call | solution.py:208
  71.1 2.6 %collective-permute-done.8.refs_3_ = f32[8,1024]{1,0:T(8,128)S(1)} collective-permute-done((f32[8,1024]{1,0:T(8,128)}, f32[8,1024]{1,0:T(8,128)S(1)}, u32[]{:S(2)}, u32[]{:S(2)}) %collective-permute-start.8) | collective-permute-done | bytes 32800 | tf_op jit(solution)/shard_map/ppermute | solution.py:503
  74.4 16.1 %attention_backward.1 = (bf16[1024,1024]{1,0:T(8,128)(2,1)}, bf16[1024,256]{1,0:T(8,128)(2,1)}) custom-call(s32[1,3]{1,0:T(1,128)} %slice.25.refs_0_, f32[8,1024]{1,0:T(8,128)} %get-tuple-element.57.refs_1_, f32[8,1024]{1,0:T(8,128)} %copy-done.13, f32[8,1024]{1,0:T(8,128)} %copy-done.14, f32[8,1024]{1,0:T(8,128)} %copy-done.15, ...), custom_call_target="tpu_custom_call" | custom-call | flops 4294967296 | bytes 15204352 | tf_op jit(solution)/shard_map/attention_backward/pallas_call | solution.py:317
  90.5 1.8 convolution_convert_fusion.4
  92.6 1.9 %collective-permute-done.10 = bf16[256,1024]{1,0:T(8,128)(2,1)} collective-permute-done((bf16[256,1024]{1,0:T(8,128)(2,1)S(1)}, bf16[256,1024]{1,0:T(8,128)(2,1)}, u32[]{:S(2)}, u32[]{:S(2)}) %collective-permute-start.10) | collective-permute-done | bytes 524320 | tf_op jit(solution)/shard_map/ppermute | solution.py:503
  94.4 2.7 %fusion.3 = bf16[256,1024]{1,0:T(8,128)(2,1)} fusion(bf16[1024,1024]{1,0:T(8,128)(2,1)S(1)} %copy-done.6, bf16[256,1024]{1,0:T(8,128)(2,1)} %collective-permute-done.10, bf16[1024,1024]{1,0:T(8,128)(2,1)} %get-tuple-element.66, s32[]{:T(128)S(6)} %select_n.192), kind=kOutput, calls=%fused_computation.13 | convolution fusion | flops 537657344 | bytes 3670020 | tf_op jit(solution)/shard_map/dot_general | solution.py:27
  97.2 1.6 convolution_convert_fusion.3
  98.9 2.4 %convolution_convert_fusion.1 = bf16[1024,1024]{1,0:T(8,128)(2,1)S(1)} fusion(bf16[1024,1024]{1,0:T(8,128)(2,1)S(1)} %copy-done.18, bf16[1024,1024]{1,0:T(8,128)(2,1)S(1)} %copy-done.17), kind=kOutput, calls=%fused_computation.2 | convolution fusion | flops 2148532224 | bytes 6291456 | tf_op jit(solution)/shard_map/dot_general | solution.py:432
  101.6 1.8 %collective-permute-start.12 = (bf16[256,1024]{1,0:T(8,128)(2,1)}, bf16[256,1024]{1,0:T(8,128)(2,1)}, u32[]{:S(2)}, u32[]{:S(2)}) collective-permute-start(bf16[256,1024]{1,0:T(8,128)(2,1)} %fusion.3), channel_id=1, source_target_pairs={{0,8},{1,9},{2,10},{3,11},{4,12},{5,13},{6,14},{7,15},{8,0},{9,1},... | collective-permute-start | bytes 1572872 | tf_op jit(solution)/shard_map/ppermute | solution.py:503
  105.9 1.6 convolution_convert_fusion.2
  112.4 3.8 %collective-permute-done.12 = bf16[256,1024]{1,0:T(8,128)(2,1)} collective-permute-done((bf16[256,1024]{1,0:T(8,128)(2,1)}, bf16[256,1024]{1,0:T(8,128)(2,1)}, u32[]{:S(2)}, u32[]{:S(2)}) %collective-permute-start.12) | collective-permute-done | bytes 524320 | tf_op jit(solution)/shard_map/ppermute | solution.py:503
  116.2 2.9 %fusion.4 = bf16[256,1024]{1,0:T(8,128)(2,1)S(1)} fusion(bf16[1024,1024]{1,0:T(8,128)(2,1)} %pad_maximum_fusion.refs_4_, bf16[256,1024]{1,0:T(8,128)(2,1)} %collective-permute-done.12, bf16[256,1024]{1,0:T(8,128)(2,1)} %collective-permute-done.11, bf16[256,1024]{1,0:T(8,128)(2,1)S(1)} %broadcast_select_fusion, bf16[1024,1024]{1,0:T(8,128)(2,1)} %get-tuple-element.66, ...), kind=kOutput, calls=%fused_computation.14 | convolution fusion | flops 538705920 | bytes 4718596 | tf_op jit(solution)/shard_map/dot_general | solution.py:27
  121.4 6.4 %collective-permute-done.14 = bf16[2,256,640]{2,1,0:T(8,128)(2,1)} collective-permute-done((bf16[2,256,640]{2,1,0:T(8,128)(2,1)}, bf16[2,256,640]{2,1,0:T(8,128)(2,1)}, u32[]{:S(2)}, u32[]{:S(2)}) %collective-permute-start.14) | collective-permute-done | bytes 655392 | tf_op jit(solution)/shard_map/ppermute | solution.py:503
  127.8 5.0 %all-to-all-start = ((bf16[32,16,1152]{2,1,0:T(8,128)(2,1)}), bf16[32,16,1152]{2,1,0:T(8,128)(2,1)S(1)}, u32[]{:S(2)}, u32[]{:S(2)}) async-start(bf16[32,16,1152]{2,1,0:T(8,128)(2,1)} %bitcast.25), calls=%async_computation | async-start | bytes 2359296 | tf_op jit(solution)/shard_map/all_to_all | solution.py:424
  135.2 1.8 collective-permute-start.16
  138.3 1.5 collective-permute-start.15
  139.8 14.1 %collective-permute-done.16 = bf16[256,640]{1,0:T(8,128)(2,1)} collective-permute-done((bf16[256,640]{1,0:T(8,128)(2,1)}, bf16[256,640]{1,0:T(8,128)(2,1)}, u32[]{:S(2)}, u32[]{:S(2)}) %collective-permute-start.16) | collective-permute-done | bytes 327712 | tf_op jit(solution)/shard_map/ppermute | solution.py:503
  156.0 3.6 %collective-permute-start.17 = (bf16[128,1024]{1,0:T(8,128)(2,1)}, bf16[128,1024]{1,0:T(8,128)(2,1)}, u32[]{:S(2)}, u32[]{:S(2)}) collective-permute-start(bf16[128,1024]{1,0:T(8,128)(2,1)} %get-tuple-element.88), channel_id=1, source_target_pairs={{0,0},{1,8},{2,2},{3,10},{4,4},{5,12},{6,6},{7,14},{8,16},{9,24},{... | collective-permute-start | bytes 786440 | tf_op jit(solution)/shard_map/ppermute | solution.py:503
  160.3 2.1 %collective-permute-start.19 = (bf16[128,256]{1,0:T(8,128)(2,1)}, bf16[128,256]{1,0:T(8,128)(2,1)}, u32[]{:S(2)}, u32[]{:S(2)}) collective-permute-start(bf16[128,256]{1,0:T(8,128)(2,1)} %get-tuple-element.92), channel_id=1, source_target_pairs={{0,0},{1,2},{2,8},{3,10},{4,16},{5,18},{6,24},{7,26},{8,4},{9,6},{... | collective-permute-start | bytes 196616 | tf_op jit(solution)/shard_map/ppermute | solution.py:503
  162.4 1.9 %collective-permute-start.20 = (bf16[128,256]{1,0:T(8,128)(2,1)}, bf16[128,256]{1,0:T(8,128)(2,1)}, u32[]{:S(2)}, u32[]{:S(2)}) collective-permute-start(bf16[128,256]{1,0:T(8,128)(2,1)} %get-tuple-element.91), channel_id=1, source_target_pairs={{0,1},{1,3},{2,9},{3,11},{4,17},{5,19},{6,25},{7,27},{8,5},{9,7},{... | collective-permute-start | bytes 196616 | tf_op jit(solution)/shard_map/ppermute | solution.py:503
  165.4 4.2 %update_rows.1 = (f32[512,1024]{1,0:T(8,128)}, f32[1,512]{1,0:T(1,128)}) custom-call(bf16[512,1152]{1,0:T(8,128)(2,1)} %bitcast.62, f32[512,1024]{1,0:T(8,128)} %table_ref.1, f32[1,512]{1,0:T(1,128)} %bitcast.75), custom_call_target="tpu_custom_call" | custom-call | flops 536870912 | bytes 5242880 | tf_op jit(solution)/shard_map/update_rows/pallas_call | solution.py:376
  169.6 6.9 %collective-permute-done.18.proj_two = bf16[128,1024]{1,0:T(8,128)(2,1)} collective-permute-done((bf16[128,1024]{1,0:T(8,128)(2,1)S(1)}, bf16[128,1024]{1,0:T(8,128)(2,1)}, u32[]{:S(2)}, u32[]{:S(2)}) %collective-permute-start.18) | collective-permute-done | bytes 262176 | tf_op jit(solution)/shard_map/ppermute | solution.py:503
  176.5 2.3 %collective-permute-done.20.out_two = bf16[128,256]{1,0:T(8,128)(2,1)} collective-permute-done((bf16[128,256]{1,0:T(8,128)(2,1)}, bf16[128,256]{1,0:T(8,128)(2,1)}, u32[]{:S(2)}, u32[]{:S(2)}) %collective-permute-start.20) | collective-permute-done | bytes 65568 | tf_op jit(solution)/shard_map/ppermute | solution.py:503
  178.9 1.9 %last_sums.1 = (f32[128,768]{1,0:T(8,128)}, f32[128,256]{1,0:T(8,128)}, f32[128,256]{1,0:T(8,128)}) custom-call(bf16[128,1024]{1,0:T(8,128)(2,1)} %collective-permute-done.17.proj_one, bf16[128,1024]{1,0:T(8,128)(2,1)} %collective-permute-done.18.proj_two, bf16[128,256]{1,0:T(8,128)(2,1)} %collective-permute-done.19.out_one, ...), custom_call_target="tpu_custom_call" | custom-call | bytes 1966080 | tf_op jit(solution)/shard_map/last_sums/pallas_call | solution.py:548
  (105 shorter events, 31.0 us)
Async XLA Ops:
  0.6 6.7 %copy-start = (bf16[1024,1024]{1,0:T(8,128)(2,1)S(1)}, bf16[1024,1024]{1,0:T(8,128)(2,1)}, u32[]{:S(2)}) copy-start(bf16[1024,1024]{1,0:T(8,128)(2,1)} %param.16) | copy-start | bytes 6291460
  0.6 13.5 %collective-permute-start = (bf16[256,1024]{1,0:T(8,128)(2,1)}, bf16[256,1024]{1,0:T(8,128)(2,1)S(1)}, u32[]{:S(2)}, u32[]{:S(2)}) collective-permute-start(bf16[256,1024]{1,0:T(8,128)(2,1)} %param.10), channel_id=1, source_target_pairs={{1,24},{3,26},{5,28},{7,30},{9,16},{11,18},{13,20},{15,22},{16,9},... | collective-permute-start | bytes 1572872 | tf_op jit(solution)/shard_map/ppermute | solution.py:503
  1.5 13.1 %collective-permute-start.1 = (bf16[256,1024]{1,0:T(8,128)(2,1)}, bf16[256,1024]{1,0:T(8,128)(2,1)}, u32[]{:S(2)}, u32[]{:S(2)}) collective-permute-start(bf16[256,1024]{1,0:T(8,128)(2,1)} %param.10), channel_id=1, source_target_pairs={{0,8},{1,16},{2,10},{3,18},{4,12},{5,20},{6,14},{7,22},{8,0},{9,24... | collective-permute-start | bytes 1572872 | tf_op jit(solution)/shard_map/ppermute | solution.py:503
  6.6 5.8 %collective-permute-start.2 = (s32[1,384]{1,0:T(1,128)S(1)}, s32[1,384]{1,0:T(1,128)S(1)}, u32[]{:S(2)}, u32[]{:S(2)}) collective-permute-start(s32[1,384]{1,0:T(1,128)S(1)} %pad_add_fusion), channel_id=1, source_target_pairs={{1,24},{3,26},{5,28},{7,30},{9,16},{11,18},{13,20},{15,22},{16,9},... | collective-permute-start | bytes 4616 | tf_op jit(solution)/shard_map/ppermute | solution.py:503
  12.4 19.7 %copy-start.11 = (bf16[256,1024]{1,0:T(8,128)(2,1)S(1)}, bf16[256,1024]{1,0:T(8,128)(2,1)}, u32[]{:S(2)}) copy-start(bf16[256,1024]{1,0:T(8,128)(2,1)} %param.11) | copy-start | bytes 1572868
  15.7 20.0 %copy-start.8 = (bf16[512,1024]{1,0:T(8,128)(2,1)}, bf16[512,1024]{1,0:T(8,128)(2,1)S(1)}, u32[]{:S(2)}) copy-start(bf16[512,1024]{1,0:T(8,128)(2,1)S(1)} %pad_maximum_fusion.1.refs_2_) | copy-start | bytes 3145732
  15.7 20.0 %collective-permute-start.3 = (bf16[512,1024]{1,0:T(8,128)(2,1)S(1)}, bf16[512,1024]{1,0:T(8,128)(2,1)}, u32[]{:S(2)}, u32[]{:S(2)}) collective-permute-start(bf16[512,1024]{1,0:T(8,128)(2,1)S(1)} %pad_maximum_fusion.1.refs_2_), channel_id=1, source_target_pairs={{0,1},{1,0},{2,3},{3,2},{4,5},{5,4},{6,7},{7,6},{8,9},{9,8},{10,11... | collective-permute-start | bytes 3145736 | tf_op jit(solution)/shard_map/ppermute | solution.py:503
  32.1 20.4 %collective-permute-start.4 = (bf16[256,1024]{1,0:T(8,128)(2,1)S(1)}, bf16[256,1024]{1,0:T(8,128)(2,1)S(1)}, u32[]{:S(2)}, u32[]{:S(2)}) collective-permute-start(bf16[256,1024]{1,0:T(8,128)(2,1)S(1)} %copy-done.11), channel_id=1, source_target_pairs={{1,24},{3,26},{5,28},{7,30},{9,16},{11,18},{13,20},{15,22},{16,9},... | collective-permute-start | bytes 1572872 | tf_op jit(solution)/shard_map/ppermute | solution.py:503
  32.8 19.7 %collective-permute-start.5 = (bf16[256,1024]{1,0:T(8,128)(2,1)S(1)}, bf16[256,1024]{1,0:T(8,128)(2,1)S(1)}, u32[]{:S(2)}, u32[]{:S(2)}) collective-permute-start(bf16[256,1024]{1,0:T(8,128)(2,1)S(1)} %copy-done.11), channel_id=1, source_target_pairs={{0,8},{1,16},{2,10},{3,18},{4,12},{5,20},{6,14},{7,22},{8,0},{9,24... | collective-permute-start | bytes 1572872 | tf_op jit(solution)/shard_map/ppermute | solution.py:503
  52.7 11.0 %copy-start.3 = (bf16[512,1024]{1,0:T(8,128)(2,1)}, bf16[512,1024]{1,0:T(8,128)(2,1)S(1)}, u32[]{:S(2)}) copy-start(bf16[512,1024]{1,0:T(8,128)(2,1)S(1)} %pad_maximum_fusion.2.refs_1_) | copy-start | bytes 3145732
  52.7 10.9 %collective-permute-start.6 = (bf16[512,1024]{1,0:T(8,128)(2,1)S(1)}, bf16[512,1024]{1,0:T(8,128)(2,1)S(1)}, u32[]{:S(2)}, u32[]{:S(2)}) collective-permute-start(bf16[512,1024]{1,0:T(8,128)(2,1)S(1)} %pad_maximum_fusion.2.refs_1_), channel_id=1, source_target_pairs={{0,1},{1,0},{2,3},{3,2},{4,5},{5,4},{6,7},{7,6},{8,9},{9,8},{10,11... | collective-permute-start | bytes 3145736 | tf_op jit(solution)/shard_map/ppermute | solution.py:503
  69.3 1.9 %collective-permute-start.7 = (f32[8,1024]{1,0:T(8,128)}, f32[8,1024]{1,0:T(8,128)S(1)}, u32[]{:S(2)}, u32[]{:S(2)}) collective-permute-start(f32[8,1024]{1,0:T(8,128)} %get-tuple-element.57.refs_1_), channel_id=1, source_target_pairs={{0,1},{1,0},{2,3},{3,2},{4,5},{5,4},{6,7},{7,6},{8,9},{9,8},{10,11... | collective-permute-start | bytes 98312 | tf_op jit(solution)/shard_map/ppermute | solution.py:503
  69.6 4.1 %collective-permute-start.8 = (f32[8,1024]{1,0:T(8,128)}, f32[8,1024]{1,0:T(8,128)S(1)}, u32[]{:S(2)}, u32[]{:S(2)}) collective-permute-start(f32[8,1024]{1,0:T(8,128)} %get-tuple-element.57.refs_1_), channel_id=1, source_target_pairs={{0,8},{1,9},{2,10},{3,11},{4,12},{5,13},{6,14},{7,15},{8,0},{9,1},... | collective-permute-start | bytes 98312 | tf_op jit(solution)/shard_map/ppermute | solution.py:503
  69.7 4.1 %collective-permute-start.9 = (f32[8,1024]{1,0:T(8,128)}, f32[8,1024]{1,0:T(8,128)S(1)}, u32[]{:S(2)}, u32[]{:S(2)}) collective-permute-start(f32[8,1024]{1,0:T(8,128)} %get-tuple-element.57.refs_1_), channel_id=1, source_target_pairs={{0,9},{1,8},{2,11},{3,10},{4,13},{5,12},{6,15},{7,14},{8,1},{9,0},... | collective-permute-start | bytes 98312 | tf_op jit(solution)/shard_map/ppermute | solution.py:503
  74.4 16.1 %copy-start.6 = (bf16[1024,1024]{1,0:T(8,128)(2,1)S(1)}, bf16[1024,1024]{1,0:T(8,128)(2,1)}, u32[]{:S(2)}) copy-start(bf16[1024,1024]{1,0:T(8,128)(2,1)} %pad_maximum_fusion.refs_4_) | copy-start | bytes 6291460
  92.3 2.1 %collective-permute-start.10 = (bf16[256,1024]{1,0:T(8,128)(2,1)S(1)}, bf16[256,1024]{1,0:T(8,128)(2,1)}, u32[]{:S(2)}, u32[]{:S(2)}) collective-permute-start(bf16[256,1024]{1,0:T(8,128)(2,1)S(1)} %convolution_convert_fusion.4), channel_id=1, source_target_pairs={{0,1},{1,0},{2,3},{3,2},{4,5},{5,4},{6,7},{7,6},{8,9},{9,8},{10,11... | collective-permute-start | bytes 1572872 | tf_op jit(solution)/shard_map/ppermute | solution.py:503
  92.6 4.6 %copy-start.17 = (bf16[1024,1024]{1,0:T(8,128)(2,1)S(1)}, bf16[1024,1024]{1,0:T(8,128)(2,1)}, u32[]{:S(2)}) copy-start(bf16[1024,1024]{1,0:T(8,128)(2,1)} %get-tuple-element.66) | copy-start | bytes 6291460
  98.8 17.5 %collective-permute-start.11 = (bf16[256,1024]{1,0:T(8,128)(2,1)}, bf16[256,1024]{1,0:T(8,128)(2,1)}, u32[]{:S(2)}, u32[]{:S(2)}) collective-permute-start(bf16[256,1024]{1,0:T(8,128)(2,1)} %convolution_convert_fusion.3), channel_id=1, source_target_pairs={{0,1},{1,0},{2,3},{3,2},{4,5},{5,4},{6,7},{7,6},{8,9},{9,8},{10,11... | collective-permute-start | bytes 1572872 | tf_op jit(solution)/shard_map/ppermute | solution.py:503
  101.5 4.3 %copy-start.5 = (bf16[1024,1024]{1,0:T(8,128)(2,1)S(1)}, bf16[1024,1024]{1,0:T(8,128)(2,1)}, u32[]{:S(2)}) copy-start(bf16[1024,1024]{1,0:T(8,128)(2,1)} %get-tuple-element.71) | copy-start | bytes 6291460
  101.5 4.3 %copy-start.12 = (bf16[1024,256]{1,0:T(8,128)(2,1)S(1)}, bf16[1024,256]{1,0:T(8,128)(2,1)}, u32[]{:S(2)}) copy-start(bf16[1024,256]{1,0:T(8,128)(2,1)} %get-tuple-element.70) | copy-start | bytes 1572868
  101.6 14.6 %collective-permute-start.12 = (bf16[256,1024]{1,0:T(8,128)(2,1)}, bf16[256,1024]{1,0:T(8,128)(2,1)}, u32[]{:S(2)}, u32[]{:S(2)}) collective-permute-start(bf16[256,1024]{1,0:T(8,128)(2,1)} %fusion.3), channel_id=1, source_target_pairs={{0,8},{1,9},{2,10},{3,11},{4,12},{5,13},{6,14},{7,15},{8,0},{9,1},... | collective-permute-start | bytes 1572872 | tf_op jit(solution)/shard_map/ppermute | solution.py:503
  104.4 17.0 %collective-permute-start.13 = (bf16[2,256,640]{2,1,0:T(8,128)(2,1)}, bf16[2,256,640]{2,1,0:T(8,128)(2,1)}, u32[]{:S(2)}, u32[]{:S(2)}) collective-permute-start(bf16[2,256,640]{2,1,0:T(8,128)(2,1)} %dynamic-slice_bitcast_fusion), channel_id=1, source_target_pairs={{0,2},{1,3},{2,0},{3,1},{4,6},{5,7},{6,4},{7,5},{8,10},{9,11},{10,... | collective-permute-start | bytes 1966088 | tf_op jit(solution)/shard_map/ppermute | solution.py:503
  111.0 16.8 %collective-permute-start.14 = (bf16[2,256,640]{2,1,0:T(8,128)(2,1)}, bf16[2,256,640]{2,1,0:T(8,128)(2,1)}, u32[]{:S(2)}, u32[]{:S(2)}) collective-permute-start(bf16[2,256,640]{2,1,0:T(8,128)(2,1)} %pad_maximum_fusion.3), channel_id=1, source_target_pairs={{0,4},{1,5},{2,6},{3,7},{4,0},{5,1},{6,2},{7,3},{8,12},{9,13},{10,... | collective-permute-start | bytes 1966088 | tf_op jit(solution)/shard_map/ppermute | solution.py:503
  112.4 6.7 %copy-start.9 = (bf16[512,256]{1,0:T(8,128)(2,1)S(1)}, bf16[512,256]{1,0:T(8,128)(2,1)}, u32[]{:S(2)}) copy-start(bf16[512,256]{1,0:T(8,128)(2,1)} %fusion.15) | copy-start | bytes 786436
  127.8 36.6 %all-to-all-start = ((bf16[32,16,1152]{2,1,0:T(8,128)(2,1)}), bf16[32,16,1152]{2,1,0:T(8,128)(2,1)S(1)}, u32[]{:S(2)}, u32[]{:S(2)}) async-start(bf16[32,16,1152]{2,1,0:T(8,128)(2,1)} %bitcast.25), calls=%async_computation | async-start | bytes 2359296 | tf_op jit(solution)/shard_map/all_to_all | solution.py:424
  135.2 18.7 %collective-permute-start.16 = (bf16[256,640]{1,0:T(8,128)(2,1)}, bf16[256,640]{1,0:T(8,128)(2,1)}, u32[]{:S(2)}, u32[]{:S(2)}) collective-permute-start(bf16[256,640]{1,0:T(8,128)(2,1)} %dynamic-slice_bitcast_fusion.3), channel_id=1, source_target_pairs={{0,2},{1,3},{2,0},{3,1},{4,6},{5,7},{6,4},{7,5},{8,10},{9,11},{10,... | collective-permute-start | bytes 983048 | tf_op jit(solution)/shard_map/ppermute | solution.py:503
  138.3 16.8 %collective-permute-start.15 = (bf16[256,640]{1,0:T(8,128)(2,1)S(1)}, bf16[256,640]{1,0:T(8,128)(2,1)S(1)}, u32[]{:S(2)}, u32[]{:S(2)}) collective-permute-start(bf16[256,640]{1,0:T(8,128)(2,1)S(1)} %dynamic-slice_bitcast_fusion.4), channel_id=1, source_target_pairs={{0,4},{1,5},{2,6},{3,7},{4,0},{5,1},{6,2},{7,3},{8,12},{9,13},{10,... | collective-permute-start | bytes 983048 | tf_op jit(solution)/shard_map/ppermute | solution.py:503
  156.0 13.6 %collective-permute-start.17 = (bf16[128,1024]{1,0:T(8,128)(2,1)}, bf16[128,1024]{1,0:T(8,128)(2,1)}, u32[]{:S(2)}, u32[]{:S(2)}) collective-permute-start(bf16[128,1024]{1,0:T(8,128)(2,1)} %get-tuple-element.88), channel_id=1, source_target_pairs={{0,0},{1,8},{2,2},{3,10},{4,4},{5,12},{6,6},{7,14},{8,16},{9,24},{... | collective-permute-start | bytes 786440 | tf_op jit(solution)/shard_map/ppermute | solution.py:503
  159.6 16.9 %collective-permute-start.18 = (bf16[128,1024]{1,0:T(8,128)(2,1)S(1)}, bf16[128,1024]{1,0:T(8,128)(2,1)}, u32[]{:S(2)}, u32[]{:S(2)}) collective-permute-start(bf16[128,1024]{1,0:T(8,128)(2,1)S(1)} %get-tuple-element.87), channel_id=1, source_target_pairs={{0,1},{1,9},{2,3},{3,11},{4,5},{5,13},{6,7},{7,15},{8,17},{9,25},{... | collective-permute-start | bytes 786440 | tf_op jit(solution)/shard_map/ppermute | solution.py:503
  159.6 21.2 %copy-start.1 = (bf16[1024,1024]{1,0:T(8,128)(2,1)S(1)}, bf16[1024,1024]{1,0:T(8,128)(2,1)}, u32[]{:S(2)}) copy-start(bf16[1024,1024]{1,0:T(8,128)(2,1)} %param.16) | copy-start | bytes 6291460
  160.3 16.3 %collective-permute-start.19 = (bf16[128,256]{1,0:T(8,128)(2,1)}, bf16[128,256]{1,0:T(8,128)(2,1)}, u32[]{:S(2)}, u32[]{:S(2)}) collective-permute-start(bf16[128,256]{1,0:T(8,128)(2,1)} %get-tuple-element.92), channel_id=1, source_target_pairs={{0,0},{1,2},{2,8},{3,10},{4,16},{5,18},{6,24},{7,26},{8,4},{9,6},{... | collective-permute-start | bytes 196616 | tf_op jit(solution)/shard_map/ppermute | solution.py:503
  162.4 16.5 %collective-permute-start.20 = (bf16[128,256]{1,0:T(8,128)(2,1)}, bf16[128,256]{1,0:T(8,128)(2,1)}, u32[]{:S(2)}, u32[]{:S(2)}) collective-permute-start(bf16[128,256]{1,0:T(8,128)(2,1)} %get-tuple-element.91), channel_id=1, source_target_pairs={{0,1},{1,3},{2,9},{3,11},{4,17},{5,19},{6,25},{7,27},{8,5},{9,7},{... | collective-permute-start | bytes 196616 | tf_op jit(solution)/shard_map/ppermute | solution.py:503
  (9 other events, 14.1 us)
where the time goes:
time: 182 us; the launch traced here: 181 us
  starting transfers between devices  55.5 us (30%)
  Pallas kernels  43.7 us (24%)
  waiting for transfers between devices  41.5 us (23%)
  matrix products  14.7 us (8%)
  local copies, waits for them, and re-layouts  13 us (7%)
  other arithmetic  11.3 us (6%)
    ppermute x21, starting transfers between devices, send(): return lax.ppermute(array, ('seq', 'dp'), steps)  50.5 us
    ppermute x21, waiting for transfers between devices, send(): return lax.ppermute(array, ('seq', 'dp'), steps)  41.5 us
    pallas_call x1, Pallas kernels, forward_attention(): pl.pallas_call(functools.partial(forward_kernel, blk=blk, users=users, ma...  16.8 us
    pallas_call x1, Pallas kernels, backward_attention(): pl.pallas_call(functools.partial(backward_kernel, blk=blk, users=users, m...  16.1 us
    dot_general x4, matrix products, dot_nt(): lax.dot_general(a, b, (((1,), (1,)), ((), ())), preferred_element_type=F32)  8.98 us
    all_to_all x1, starting transfers between devices, to_owners(): lax.all_to_all(rows.reshape(shape), ('seq', 'dp'), split_axis=0, concat_a...  5.05 us
    pallas_call x1, Pallas kernels, event_stats(): pl.pallas_call(functools.partial(stats_kernel, blk=blk, count=count), in_...  4.61 us
    pallas_call x1, Pallas kernels, update_rows(): pl.pallas_call(update_kernel, grid=(rows_own // blk,), in_specs=[pl.Block...  4.19 us
  transfers between devices with their start and end apart: 22, of which 10 were waited for; matrix products, arithmetic and copies ran while one was open for 16% of the time, Pallas kernels for 12%

commit v1 on v0

--- a/solution.py
+++ b/solution.py
@@ -535,6 +535,28 @@
     return lax.optimization_barrier(arrays)
 
 
+def merge_kernel(yx_ref, a_kept, a_got, b_kept, b_got, a_next, a_sent, b_next, b_sent):
+    for bit, kept, got, following, sent in (
+        (yx_ref[0], a_kept, a_got, a_next, a_sent),
+        (yx_ref[1], b_kept, b_got, b_next, b_sent),
+    ):
+        following[...] = (kept[bit].astype(F32) + got[bit].astype(F32)).astype(BF)
+        sent[...] = (kept[1 - bit].astype(F32) + got[1 - bit].astype(F32)).astype(BF)
+
+
+def merge_halves(yx, a_kept, a_got, b_kept, b_got):
+    out = jax.ShapeDtypeStruct(a_kept.shape[1:], BF)
+    return pl.pallas_call(
+        merge_kernel,
+        in_specs=[pl.BlockSpec(memory_space=pltpu.SMEM)] + [pl.BlockSpec(memory_space=pltpu.VMEM)] * 4,
+        out_specs=[pl.BlockSpec(memory_space=pltpu.VMEM)] * 4,
+        out_shape=[out] * 4,
+        compiler_params=pltpu.CompilerParams(vmem_limit_bytes=VMEM_LIMIT),
+        cost_estimate=pl.CostEstimate(flops=0, bytes_accessed=12_000_000, transcendentals=0),
+        name="merge_halves",
+    )(yx, a_kept, a_got, b_kept, b_got)
+
+
 def sums_kernel(proj_one, proj_two, out_one, out_two, attn_ref, gate_ref, out_ref):
     cut = attn_ref.shape[1]
     attn_ref[...] = proj_one[:, :cut].astype(F32) + proj_two[:, :cut].astype(F32)
@@ -650,13 +672,10 @@
     input_grad = input_grad + from_core.astype(F32) + from_near.astype(F32)
     rows = jnp.concatenate([input_grad.astype(BF), numbers], axis=1)
     rows = jnp.dot(slot_matrix, rows, preferred_element_type=F32).astype(BF)
-    rows, a_got, b_got = tie(rows, a_got, b_got)
     got_rows = to_owners(rows, devices, capacity)
 
-    a = (a_kept.astype(F32) + a_got.astype(F32)).astype(BF)
-    b = (b_kept.astype(F32) + b_got.astype(F32)).astype(BF)
-    a_kept, a_sent = halves(a, y, 0)
-    b_kept, b_sent = halves(b, x, 0)
+    yx = jnp.stack([y, x]).astype(jnp.int32)
+    a_kept, a_sent, b_kept, b_sent = merge_halves(yx, a_kept, a_got, b_kept, b_got)
     a = (a_kept.astype(F32) + swap_y(a_sent).astype(F32)).astype(BF)
     b = (b_kept.astype(F32) + swap_x(b_sent).astype(F32)).astype(BF)
 

time: 182 us -> 193 us (1.060)
  waiting for transfers between devices: 41.5 us -> 53.1 us
  Pallas kernels: 43.7 us -> 46.3 us
    ppermute x21, waiting for transfers between devices: 41.5 us -> 53.1 us  [send(): return lax.ppermute(array, ('seq', 'dp'), steps)]
    pallas_call x0 -> x1, Pallas kernels: none -> 2.81 us  [merge_halves(): pl.pallas_call(merge_kernel, in_specs=[pl.BlockSpec(memory_space=pltpu.SM...]
    convert_element_type x2 -> x0, other arithmetic: 2.6 us -> none  [the longest x1 1.35 us: body_pairs(): b = (b_kept.astype(F32) + b_got.astype(F32)).astype(BF)]
  transfers between devices with their start and end apart: 22 -> 22, of which waited for: 10 -> 10; matrix products, arithmetic and copies ran while one was open for 16% -> 13% of each run, Pallas kernels for 12% -> 12%
where the time goes in v1:
time: 193 us; the launch traced here: 192 us
  starting transfers between devices  54.5 us (28%)
  waiting for transfers between devices  53.1 us (28%)
  Pallas kernels  46.3 us (24%)
  matrix products  14.1 us (7%)
  local copies, waits for them, and re-layouts  12.4 us (6%)
  other arithmetic  10.2 us (5%)
    ppermute x21, waiting for transfers between devices, send(): return lax.ppermute(array, ('seq', 'dp'), steps)  53.1 us
    ppermute x21, starting transfers between devices, send(): return lax.ppermute(array, ('seq', 'dp'), steps)  49.2 us
    pallas_call x1, Pallas kernels, forward_attention(): pl.pallas_call(functools.partial(forward_kernel, blk=blk, users=users, ma...  16.8 us
    pallas_call x1, Pallas kernels, backward_attention(): pl.pallas_call(functools.partial(backward_kernel, blk=blk, users=users, m...  16.1 us
    dot_general x4, matrix products, dot_nt(): lax.dot_general(a, b, (((1,), (1,)), ((), ())), preferred_element_type=F32)  8.41 us
    all_to_all x1, starting transfers between devices, to_owners(): lax.all_to_all(rows.reshape(shape), ('seq', 'dp'), split_axis=0, concat_a...  5.33 us
    pallas_call x1, Pallas kernels, event_stats(): pl.pallas_call(functools.partial(stats_kernel, blk=blk, count=count), in_...  4.57 us
    pallas_call x1, Pallas kernels, update_rows(): pl.pallas_call(update_kernel, grid=(rows_own // blk,), in_specs=[pl.Block...  4.19 us
  transfers between devices with their start and end apart: 22, of which 10 were waited for; matrix products, arithmetic and copies ran while one was open for 13% of the time, Pallas kernels for 12%

profile of v1, /device:TPU:0, one launch (start us, length us, event | category | flops | bytes accessed | tf_op | source)
XLA Modules:
  0.0 191.7 jit_solution(12046494778311679080)
XLA Ops:
  1.5 3.1 %collective-permute-start.1 = (bf16[256,1024]{1,0:T(8,128)(2,1)}, bf16[256,1024]{1,0:T(8,128)(2,1)}, u32[]{:S(2)}, u32[]{:S(2)}) collective-permute-start(bf16[256,1024]{1,0:T(8,128)(2,1)} %param.10), channel_id=1, source_target_pairs={{0,8},{1,16},{2,10},{3,18},{4,12},{5,20},{6,14},{7,22},{8,0},{9,24... | collective-permute-start | bytes 1572872 | tf_op jit(solution)/shard_map/ppermute | solution.py:503
  7.4 1.9 constant_dynamic-slice_fusion.2.refs_3_
  10.8 1.6 pad_maximum_fusion.refs_4_
  15.7 16.4 %collective-permute-start.3 = (bf16[512,1024]{1,0:T(8,128)(2,1)S(1)}, bf16[512,1024]{1,0:T(8,128)(2,1)}, u32[]{:S(2)}, u32[]{:S(2)}) collective-permute-start(bf16[512,1024]{1,0:T(8,128)(2,1)S(1)} %pad_maximum_fusion.1.refs_2_), channel_id=1, source_target_pairs={{0,1},{1,0},{2,3},{3,2},{4,5},{5,4},{6,7},{7,6},{8,9},{9,8},{10,11... | collective-permute-start | bytes 3145736 | tf_op jit(solution)/shard_map/ppermute | solution.py:503
  32.8 2.3 %collective-permute-start.5 = (bf16[256,1024]{1,0:T(8,128)(2,1)S(1)}, bf16[256,1024]{1,0:T(8,128)(2,1)S(1)}, u32[]{:S(2)}, u32[]{:S(2)}) collective-permute-start(bf16[256,1024]{1,0:T(8,128)(2,1)S(1)} %copy-done.12), channel_id=1, source_target_pairs={{0,8},{1,16},{2,10},{3,18},{4,12},{5,20},{6,14},{7,22},{8,0},{9,24... | collective-permute-start | bytes 1572872 | tf_op jit(solution)/shard_map/ppermute | solution.py:503
  35.7 16.8 %attention_forward.1 = (bf16[1024,1024]{1,0:T(8,128)(2,1)}, bf16[1024,1024]{1,0:T(8,128)(2,1)}, bf16[1024,1024]{1,0:T(8,128)(2,1)}, f32[1024,256]{1,0:T(8,128)},...) custom-call(s32[1,3]{1,0:T(1,128)} %slice.25.refs_0_, ...), custom_call_target="tpu_custom_call" | custom-call | flops 4294967296 | bytes 12582912 | tf_op jit(solution)/shard_map/attention_forward/pallas_call | solution.py:150
  52.6 8.7 %collective-permute-start.6 = (bf16[512,1024]{1,0:T(8,128)(2,1)S(1)}, bf16[512,1024]{1,0:T(8,128)(2,1)S(1)}, u32[]{:S(2)}, u32[]{:S(2)}) collective-permute-start(bf16[512,1024]{1,0:T(8,128)(2,1)S(1)} %pad_maximum_fusion.2.refs_1_), channel_id=1, source_target_pairs={{0,1},{1,0},{2,3},{3,2},{4,5},{5,4},{6,7},{7,6},{8,9},{9,8},{10,11... | collective-permute-start | bytes 3145736 | tf_op jit(solution)/shard_map/ppermute | solution.py:503
  61.4 2.3 %collective-permute-done.6.refs_2_ = bf16[512,1024]{1,0:T(8,128)(2,1)S(1)} collective-permute-done((bf16[512,1024]{1,0:T(8,128)(2,1)S(1)}, bf16[512,1024]{1,0:T(8,128)(2,1)S(1)}, u32[]{:S(2)}, u32[]{:S(2)}) %collective-permute-start.6) | collective-permute-done | bytes 1048608 | tf_op jit(solution)/shard_map/ppermute | solution.py:503
  64.7 4.6 %event_stats.1 = (bf16[1024,1024]{1,0:T(8,128)(2,1)}, f32[1024,256]{1,0:T(8,128)}, f32[8,1024]{1,0:T(8,128)}) custom-call(s32[4]{0:T(128)} %pad_add_fusion.2.refs_1_.refs_0_, bf16[512,1024]{1,0:T(8,128)(2,1)} %copy-done.3, bf16[512,1024]{1,0:T(8,128)(2,1)} %copy-done.7, bf16[256,1024]{1,0:T(8,128)(2,1)} %constant_dynamic-slice_fusion.2.refs_3_, ...), custom_call_target="tpu_custom_call" | custom-call | flops 536870912 | bytes 6815744 | tf_op jit(solution)/shard_map/event_stats/pallas_call | solution.py:208
  71.1 2.6 %collective-permute-done.8.refs_3_ = f32[8,1024]{1,0:T(8,128)S(1)} collective-permute-done((f32[8,1024]{1,0:T(8,128)}, f32[8,1024]{1,0:T(8,128)S(1)}, u32[]{:S(2)}, u32[]{:S(2)}) %collective-permute-start.8) | collective-permute-done | bytes 32800 | tf_op jit(solution)/shard_map/ppermute | solution.py:503
  74.3 16.1 %attention_backward.1 = (bf16[1024,1024]{1,0:T(8,128)(2,1)}, bf16[1024,256]{1,0:T(8,128)(2,1)}) custom-call(s32[1,3]{1,0:T(1,128)} %slice.25.refs_0_, f32[8,1024]{1,0:T(8,128)} %get-tuple-element.58.refs_1_, f32[8,1024]{1,0:T(8,128)} %copy-done.14, f32[8,1024]{1,0:T(8,128)} %copy-done.15, f32[8,1024]{1,0:T(8,128)} %copy-done.16, ...), custom_call_target="tpu_custom_call" | custom-call | flops 4294967296 | bytes 15204352 | tf_op jit(solution)/shard_map/attention_backward/pallas_call | solution.py:317
  90.5 1.8 convolution_convert_fusion.4
  92.5 1.8 collective-permute-done.10
  94.2 2.6 %fusion.2 = bf16[256,1024]{1,0:T(8,128)(2,1)} fusion(bf16[1024,1024]{1,0:T(8,128)(2,1)S(1)} %copy-done.5, bf16[256,1024]{1,0:T(8,128)(2,1)S(1)} %collective-permute-done.10, bf16[1024,1024]{1,0:T(8,128)(2,1)} %get-tuple-element.67, s32[]{:T(128)S(6)} %select_n.190), kind=kOutput, calls=%fused_computation.10 | convolution fusion | flops 537657344 | bytes 3670020 | tf_op jit(solution)/shard_map/dot_general | solution.py:27
  96.9 1.6 convolution_convert_fusion.3
  98.6 1.7 collective-permute-start.18
  100.4 2.4 %convolution_convert_fusion.1 = bf16[1024,1024]{1,0:T(8,128)(2,1)S(1)} fusion(bf16[1024,1024]{1,0:T(8,128)(2,1)S(1)} %copy-done.19, bf16[1024,1024]{1,0:T(8,128)(2,1)S(1)} %copy-done.18), kind=kOutput, calls=%fused_computation.2 | convolution fusion | flops 2148532224 | bytes 6291456 | tf_op jit(solution)/shard_map/dot_general | solution.py:432
  105.8 1.5 convolution_convert_fusion.2
  108.7 4.4 %collective-permute-done.18 = bf16[256,1024]{1,0:T(8,128)(2,1)} collective-permute-done((bf16[256,1024]{1,0:T(8,128)(2,1)}, bf16[256,1024]{1,0:T(8,128)(2,1)}, u32[]{:S(2)}, u32[]{:S(2)}) %collective-permute-start.18) | collective-permute-done | bytes 524320 | tf_op jit(solution)/shard_map/ppermute | solution.py:503
  113.1 2.4 %fusion.3 = bf16[256,1024]{1,0:T(8,128)(2,1)S(1)} fusion(bf16[1024,1024]{1,0:T(8,128)(2,1)S(1)} %copy-done.5, bf16[256,1024]{1,0:T(8,128)(2,1)} %collective-permute-done.18, bf16[256,1024]{1,0:T(8,128)(2,1)} %collective-permute-done.17, bf16[256,1024]{1,0:T(8,128)(2,1)} %copy-done.6, bf16[1024,1024]{1,0:T(8,128)(2,1)} %get-tuple-element.67, s32[]{:T(128)S(6)} %select_n.199), kind=kOutput, calls=%fused_computation.11 | convolution fusion | flops 538705920 | bytes 4718596 | tf_op jit(solution)/shard_map/dot_general | solution.py:27
  115.5 1.5 convolution_convert_fusion
  117.1 5.3 %all-to-all-start = ((bf16[32,16,1152]{2,1,0:T(8,128)(2,1)}), bf16[32,16,1152]{2,1,0:T(8,128)(2,1)S(1)}, u32[]{:S(2)}, u32[]{:S(2)}) async-start(bf16[32,16,1152]{2,1,0:T(8,128)(2,1)} %bitcast.23), calls=%async_computation | async-start | bytes 2359296 | tf_op jit(solution)/shard_map/all_to_all | solution.py:424
  123.0 1.8 collective-permute-start.12
  126.3 25.6 %collective-permute-done.12.b_got = bf16[2,256,640]{2,1,0:T(8,128)(2,1)S(1)} collective-permute-done((bf16[2,256,640]{2,1,0:T(8,128)(2,1)S(1)}, bf16[2,256,640]{2,1,0:T(8,128)(2,1)S(1)}, u32[]{:S(2)}, u32[]{:S(2)}) %collective-permute-start.12) | collective-permute-done | bytes 655392 | tf_op jit(solution)/shard_map/ppermute | solution.py:503
  152.8 2.8 %merge_halves.1 = (bf16[256,640]{1,0:T(8,128)(2,1)}, bf16[256,640]{1,0:T(8,128)(2,1)}, bf16[256,640]{1,0:T(8,128)(2,1)}, bf16[256,640]{1,0:T(8,128)(2,1)}) custom-call(s32[2]{0:T(128)} %pad_add_fusion.1.yx_ref, bf16[2,256,640]{2,1,0:T(8,128)(2,1)} %get-tuple-element.88.a_kept, bf16[2,256,640]{2,1,0:T(8,128)(2,1)} %collective-permute-done.11.a_got, ...), custom_call_target="tpu_custom_call" | custom-call | bytes 12000000 | tf_op jit(solution)/shard_map/merge_halves/pallas_call | solution.py:549
  157.1 8.0 %collective-permute-done.14 = bf16[256,640]{1,0:T(8,128)(2,1)S(1)} collective-permute-done((bf16[256,640]{1,0:T(8,128)(2,1)}, bf16[256,640]{1,0:T(8,128)(2,1)S(1)}, u32[]{:S(2)}, u32[]{:S(2)}) %collective-permute-start.14) | collective-permute-done | bytes 327712 | tf_op jit(solution)/shard_map/ppermute | solution.py:503
  168.5 3.6 %collective-permute-start.15 = (bf16[128,1024]{1,0:T(8,128)(2,1)}, bf16[128,1024]{1,0:T(8,128)(2,1)}, u32[]{:S(2)}, u32[]{:S(2)}) collective-permute-start(bf16[128,1024]{1,0:T(8,128)(2,1)} %get-tuple-element.92), channel_id=1, source_target_pairs={{0,0},{1,8},{2,2},{3,10},{4,4},{5,12},{6,6},{7,14},{8,16},{9,24},{... | collective-permute-start | bytes 786440 | tf_op jit(solution)/shard_map/ppermute | solution.py:503
  172.7 2.1 %collective-permute-start.19 = (bf16[128,256]{1,0:T(8,128)(2,1)}, bf16[128,256]{1,0:T(8,128)(2,1)}, u32[]{:S(2)}, u32[]{:S(2)}) collective-permute-start(bf16[128,256]{1,0:T(8,128)(2,1)} %get-tuple-element.96), channel_id=1, source_target_pairs={{0,0},{1,2},{2,8},{3,10},{4,16},{5,18},{6,24},{7,26},{8,4},{9,6},{... | collective-permute-start | bytes 196616 | tf_op jit(solution)/shard_map/ppermute | solution.py:503
  174.9 2.0 %collective-permute-start.20 = (bf16[128,256]{1,0:T(8,128)(2,1)}, bf16[128,256]{1,0:T(8,128)(2,1)}, u32[]{:S(2)}, u32[]{:S(2)}) collective-permute-start(bf16[128,256]{1,0:T(8,128)(2,1)} %get-tuple-element.95), channel_id=1, source_target_pairs={{0,1},{1,3},{2,9},{3,11},{4,17},{5,19},{6,25},{7,27},{8,5},{9,7},{... | collective-permute-start | bytes 196616 | tf_op jit(solution)/shard_map/ppermute | solution.py:503
  178.0 4.2 %update_rows.1 = (f32[512,1024]{1,0:T(8,128)}, f32[1,512]{1,0:T(1,128)}) custom-call(bf16[512,1152]{1,0:T(8,128)(2,1)} %bitcast.53, f32[512,1024]{1,0:T(8,128)} %table_ref.1, f32[1,512]{1,0:T(1,128)} %bitcast.66), custom_call_target="tpu_custom_call" | custom-call | flops 536870912 | bytes 5242880 | tf_op jit(solution)/shard_map/update_rows/pallas_call | solution.py:376
  182.2 6.3 %collective-permute-done.16.proj_two = bf16[128,1024]{1,0:T(8,128)(2,1)} collective-permute-done((bf16[128,1024]{1,0:T(8,128)(2,1)S(1)}, bf16[128,1024]{1,0:T(8,128)(2,1)}, u32[]{:S(2)}, u32[]{:S(2)}) %collective-permute-start.16) | collective-permute-done | bytes 262176 | tf_op jit(solution)/shard_map/ppermute | solution.py:503
  189.8 1.9 last_sums.1
  (106 shorter events, 28.9 us)
Async XLA Ops:
  0.6 6.7 %copy-start = (bf16[1024,1024]{1,0:T(8,128)(2,1)S(1)}, bf16[1024,1024]{1,0:T(8,128)(2,1)}, u32[]{:S(2)}) copy-start(bf16[1024,1024]{1,0:T(8,128)(2,1)} %param.16) | copy-start | bytes 6291460
  0.6 13.5 %collective-permute-start = (bf16[256,1024]{1,0:T(8,128)(2,1)}, bf16[256,1024]{1,0:T(8,128)(2,1)S(1)}, u32[]{:S(2)}, u32[]{:S(2)}) collective-permute-start(bf16[256,1024]{1,0:T(8,128)(2,1)} %param.10), channel_id=1, source_target_pairs={{1,24},{3,26},{5,28},{7,30},{9,16},{11,18},{13,20},{15,22},{16,9},... | collective-permute-start | bytes 1572872 | tf_op jit(solution)/shard_map/ppermute | solution.py:503
  1.5 13.1 %collective-permute-start.1 = (bf16[256,1024]{1,0:T(8,128)(2,1)}, bf16[256,1024]{1,0:T(8,128)(2,1)}, u32[]{:S(2)}, u32[]{:S(2)}) collective-permute-start(bf16[256,1024]{1,0:T(8,128)(2,1)} %param.10), channel_id=1, source_target_pairs={{0,8},{1,16},{2,10},{3,18},{4,12},{5,20},{6,14},{7,22},{8,0},{9,24... | collective-permute-start | bytes 1572872 | tf_op jit(solution)/shard_map/ppermute | solution.py:503
  6.6 5.8 %collective-permute-start.2 = (s32[1,384]{1,0:T(1,128)S(1)}, s32[1,384]{1,0:T(1,128)S(1)}, u32[]{:S(2)}, u32[]{:S(2)}) collective-permute-start(s32[1,384]{1,0:T(1,128)S(1)} %pad_add_fusion), channel_id=1, source_target_pairs={{1,24},{3,26},{5,28},{7,30},{9,16},{11,18},{13,20},{15,22},{16,9},... | collective-permute-start | bytes 4616 | tf_op jit(solution)/shard_map/ppermute | solution.py:503
  10.8 3.8 %copy-start.11 = (bf16[256,1024]{1,0:T(8,128)(2,1)S(1)}, bf16[256,1024]{1,0:T(8,128)(2,1)}, u32[]{:S(2)}) copy-start(bf16[256,1024]{1,0:T(8,128)(2,1)} %param.10) | copy-start | bytes 1572868
  12.4 19.7 %copy-start.12 = (bf16[256,1024]{1,0:T(8,128)(2,1)S(1)}, bf16[256,1024]{1,0:T(8,128)(2,1)}, u32[]{:S(2)}) copy-start(bf16[256,1024]{1,0:T(8,128)(2,1)} %param.11) | copy-start | bytes 1572868
  15.7 20.0 %copy-start.8 = (bf16[512,1024]{1,0:T(8,128)(2,1)}, bf16[512,1024]{1,0:T(8,128)(2,1)S(1)}, u32[]{:S(2)}) copy-start(bf16[512,1024]{1,0:T(8,128)(2,1)S(1)} %pad_maximum_fusion.1.refs_2_) | copy-start | bytes 3145732
  15.7 20.0 %collective-permute-start.3 = (bf16[512,1024]{1,0:T(8,128)(2,1)S(1)}, bf16[512,1024]{1,0:T(8,128)(2,1)}, u32[]{:S(2)}, u32[]{:S(2)}) collective-permute-start(bf16[512,1024]{1,0:T(8,128)(2,1)S(1)} %pad_maximum_fusion.1.refs_2_), channel_id=1, source_target_pairs={{0,1},{1,0},{2,3},{3,2},{4,5},{5,4},{6,7},{7,6},{8,9},{9,8},{10,11... | collective-permute-start | bytes 3145736 | tf_op jit(solution)/shard_map/ppermute | solution.py:503
  32.1 20.3 %collective-permute-start.4 = (bf16[256,1024]{1,0:T(8,128)(2,1)S(1)}, bf16[256,1024]{1,0:T(8,128)(2,1)S(1)}, u32[]{:S(2)}, u32[]{:S(2)}) collective-permute-start(bf16[256,1024]{1,0:T(8,128)(2,1)S(1)} %copy-done.12), channel_id=1, source_target_pairs={{1,24},{3,26},{5,28},{7,30},{9,16},{11,18},{13,20},{15,22},{16,9},... | collective-permute-start | bytes 1572872 | tf_op jit(solution)/shard_map/ppermute | solution.py:503
  32.8 19.6 %collective-permute-start.5 = (bf16[256,1024]{1,0:T(8,128)(2,1)S(1)}, bf16[256,1024]{1,0:T(8,128)(2,1)S(1)}, u32[]{:S(2)}, u32[]{:S(2)}) collective-permute-start(bf16[256,1024]{1,0:T(8,128)(2,1)S(1)} %copy-done.12), channel_id=1, source_target_pairs={{0,8},{1,16},{2,10},{3,18},{4,12},{5,20},{6,14},{7,22},{8,0},{9,24... | collective-permute-start | bytes 1572872 | tf_op jit(solution)/shard_map/ppermute | solution.py:503
  52.5 11.1 %copy-start.6 = (bf16[256,1024]{1,0:T(8,128)(2,1)}, bf16[256,1024]{1,0:T(8,128)(2,1)S(1)}, u32[]{:S(2)}) copy-start(bf16[256,1024]{1,0:T(8,128)(2,1)S(1)} %broadcast_select_fusion) | copy-start | bytes 1572868
  52.6 11.0 %copy-start.3 = (bf16[512,1024]{1,0:T(8,128)(2,1)}, bf16[512,1024]{1,0:T(8,128)(2,1)S(1)}, u32[]{:S(2)}) copy-start(bf16[512,1024]{1,0:T(8,128)(2,1)S(1)} %pad_maximum_fusion.2.refs_1_) | copy-start | bytes 3145732
  52.6 11.0 %collective-permute-start.6 = (bf16[512,1024]{1,0:T(8,128)(2,1)S(1)}, bf16[512,1024]{1,0:T(8,128)(2,1)S(1)}, u32[]{:S(2)}, u32[]{:S(2)}) collective-permute-start(bf16[512,1024]{1,0:T(8,128)(2,1)S(1)} %pad_maximum_fusion.2.refs_1_), channel_id=1, source_target_pairs={{0,1},{1,0},{2,3},{3,2},{4,5},{5,4},{6,7},{7,6},{8,9},{9,8},{10,11... | collective-permute-start | bytes 3145736 | tf_op jit(solution)/shard_map/ppermute | solution.py:503
  69.2 1.9 collective-permute-start.7
  69.6 4.1 %collective-permute-start.8 = (f32[8,1024]{1,0:T(8,128)}, f32[8,1024]{1,0:T(8,128)S(1)}, u32[]{:S(2)}, u32[]{:S(2)}) collective-permute-start(f32[8,1024]{1,0:T(8,128)} %get-tuple-element.58.refs_1_), channel_id=1, source_target_pairs={{0,8},{1,9},{2,10},{3,11},{4,12},{5,13},{6,14},{7,15},{8,0},{9,1},... | collective-permute-start | bytes 98312 | tf_op jit(solution)/shard_map/ppermute | solution.py:503
  69.6 4.1 %collective-permute-start.9 = (f32[8,1024]{1,0:T(8,128)}, f32[8,1024]{1,0:T(8,128)S(1)}, u32[]{:S(2)}, u32[]{:S(2)}) collective-permute-start(f32[8,1024]{1,0:T(8,128)} %get-tuple-element.58.refs_1_), channel_id=1, source_target_pairs={{0,9},{1,8},{2,11},{3,10},{4,13},{5,12},{6,15},{7,14},{8,1},{9,0},... | collective-permute-start | bytes 98312 | tf_op jit(solution)/shard_map/ppermute | solution.py:503
  74.3 16.1 %copy-start.5 = (bf16[1024,1024]{1,0:T(8,128)(2,1)S(1)}, bf16[1024,1024]{1,0:T(8,128)(2,1)}, u32[]{:S(2)}) copy-start(bf16[1024,1024]{1,0:T(8,128)(2,1)} %pad_maximum_fusion.refs_4_) | copy-start | bytes 6291460
  92.3 2.0 %collective-permute-start.10 = (bf16[256,1024]{1,0:T(8,128)(2,1)S(1)}, bf16[256,1024]{1,0:T(8,128)(2,1)S(1)}, u32[]{:S(2)}, u32[]{:S(2)}) collective-permute-start(bf16[256,1024]{1,0:T(8,128)(2,1)S(1)} %convolution_convert_fusion.4), channel_id=1, source_target_pairs={{0,1},{1,0},{2,3},{3,2},{4,5},{5,4},{6,7},{7,6},{8,9},{9,8},{10,11... | collective-permute-start | bytes 1572872 | tf_op jit(solution)/shard_map/ppermute | solution.py:503
  92.5 4.4 %copy-start.18 = (bf16[1024,1024]{1,0:T(8,128)(2,1)S(1)}, bf16[1024,1024]{1,0:T(8,128)(2,1)}, u32[]{:S(2)}) copy-start(bf16[1024,1024]{1,0:T(8,128)(2,1)} %get-tuple-element.67) | copy-start | bytes 6291460
  98.5 14.7 %collective-permute-start.17 = (bf16[256,1024]{1,0:T(8,128)(2,1)}, bf16[256,1024]{1,0:T(8,128)(2,1)}, u32[]{:S(2)}, u32[]{:S(2)}) collective-permute-start(bf16[256,1024]{1,0:T(8,128)(2,1)} %convolution_convert_fusion.3), channel_id=1, source_target_pairs={{0,1},{1,0},{2,3},{3,2},{4,5},{5,4},{6,7},{7,6},{8,9},{9,8},{10,11... | collective-permute-start | bytes 1572872 | tf_op jit(solution)/shard_map/ppermute | solution.py:503
  98.6 14.5 %collective-permute-start.18 = (bf16[256,1024]{1,0:T(8,128)(2,1)}, bf16[256,1024]{1,0:T(8,128)(2,1)}, u32[]{:S(2)}, u32[]{:S(2)}) collective-permute-start(bf16[256,1024]{1,0:T(8,128)(2,1)} %fusion.2), channel_id=1, source_target_pairs={{0,8},{1,9},{2,10},{3,11},{4,12},{5,13},{6,14},{7,15},{8,0},{9,1},... | collective-permute-start | bytes 1572872 | tf_op jit(solution)/shard_map/ppermute | solution.py:503
  104.3 22.1 %collective-permute-start.11 = (bf16[2,256,640]{2,1,0:T(8,128)(2,1)}, bf16[2,256,640]{2,1,0:T(8,128)(2,1)}, u32[]{:S(2)}, u32[]{:S(2)}) collective-permute-start(bf16[2,256,640]{2,1,0:T(8,128)(2,1)} %get-tuple-element.87), channel_id=1, source_target_pairs={{0,2},{1,3},{2,0},{3,1},{4,6},{5,7},{6,4},{7,5},{8,10},{9,11},{10,... | collective-permute-start | bytes 1966088 | tf_op jit(solution)/shard_map/ppermute | solution.py:503
  108.7 6.8 %copy-start.9 = (bf16[512,256]{1,0:T(8,128)(2,1)S(1)}, bf16[512,256]{1,0:T(8,128)(2,1)}, u32[]{:S(2)}) copy-start(bf16[512,256]{1,0:T(8,128)(2,1)} %fusion.12) | copy-start | bytes 786436
  117.1 59.8 %all-to-all-start = ((bf16[32,16,1152]{2,1,0:T(8,128)(2,1)}), bf16[32,16,1152]{2,1,0:T(8,128)(2,1)S(1)}, u32[]{:S(2)}, u32[]{:S(2)}) async-start(bf16[32,16,1152]{2,1,0:T(8,128)(2,1)} %bitcast.23), calls=%async_computation | async-start | bytes 2359296 | tf_op jit(solution)/shard_map/all_to_all | solution.py:424
  123.0 29.0 %collective-permute-start.12 = (bf16[2,256,640]{2,1,0:T(8,128)(2,1)S(1)}, bf16[2,256,640]{2,1,0:T(8,128)(2,1)S(1)}, u32[]{:S(2)}, u32[]{:S(2)}) collective-permute-start(bf16[2,256,640]{2,1,0:T(8,128)(2,1)S(1)} %pad_maximum_fusion.4), channel_id=1, source_target_pairs={{0,4},{1,5},{2,6},{3,7},{4,0},{5,1},{6,2},{7,3},{8,12},{9,13},{10,... | collective-permute-start | bytes 1966088 | tf_op jit(solution)/shard_map/ppermute | solution.py:503
  155.6 9.5 %collective-permute-start.14 = (bf16[256,640]{1,0:T(8,128)(2,1)}, bf16[256,640]{1,0:T(8,128)(2,1)S(1)}, u32[]{:S(2)}, u32[]{:S(2)}) collective-permute-start(bf16[256,640]{1,0:T(8,128)(2,1)} %get-tuple-element.73), channel_id=1, source_target_pairs={{0,2},{1,3},{2,0},{3,1},{4,6},{5,7},{6,4},{7,5},{8,10},{9,11},{10,... | collective-permute-start | bytes 983048 | tf_op jit(solution)/shard_map/ppermute | solution.py:503
  157.1 9.5 %collective-permute-start.13 = (bf16[256,640]{1,0:T(8,128)(2,1)}, bf16[256,640]{1,0:T(8,128)(2,1)S(1)}, u32[]{:S(2)}, u32[]{:S(2)}) collective-permute-start(bf16[256,640]{1,0:T(8,128)(2,1)} %get-tuple-element.71), channel_id=1, source_target_pairs={{0,4},{1,5},{2,6},{3,7},{4,0},{5,1},{6,2},{7,3},{8,12},{9,13},{10,... | collective-permute-start | bytes 983048 | tf_op jit(solution)/shard_map/ppermute | solution.py:503
  168.5 13.7 %collective-permute-start.15 = (bf16[128,1024]{1,0:T(8,128)(2,1)}, bf16[128,1024]{1,0:T(8,128)(2,1)}, u32[]{:S(2)}, u32[]{:S(2)}) collective-permute-start(bf16[128,1024]{1,0:T(8,128)(2,1)} %get-tuple-element.92), channel_id=1, source_target_pairs={{0,0},{1,8},{2,2},{3,10},{4,4},{5,12},{6,6},{7,14},{8,16},{9,24},{... | collective-permute-start | bytes 786440 | tf_op jit(solution)/shard_map/ppermute | solution.py:503
  172.0 16.4 %collective-permute-start.16 = (bf16[128,1024]{1,0:T(8,128)(2,1)S(1)}, bf16[128,1024]{1,0:T(8,128)(2,1)}, u32[]{:S(2)}, u32[]{:S(2)}) collective-permute-start(bf16[128,1024]{1,0:T(8,128)(2,1)S(1)} %get-tuple-element.91), channel_id=1, source_target_pairs={{0,1},{1,9},{2,3},{3,11},{4,5},{5,13},{6,7},{7,15},{8,17},{9,25},{... | collective-permute-start | bytes 786440 | tf_op jit(solution)/shard_map/ppermute | solution.py:503
  172.1 19.6 %copy-start.1 = (bf16[1024,1024]{1,0:T(8,128)(2,1)S(1)}, bf16[1024,1024]{1,0:T(8,128)(2,1)}, u32[]{:S(2)}) copy-start(bf16[1024,1024]{1,0:T(8,128)(2,1)} %param.16) | copy-start | bytes 6291460
  172.7 15.7 %collective-permute-start.19 = (bf16[128,256]{1,0:T(8,128)(2,1)}, bf16[128,256]{1,0:T(8,128)(2,1)}, u32[]{:S(2)}, u32[]{:S(2)}) collective-permute-start(bf16[128,256]{1,0:T(8,128)(2,1)} %get-tuple-element.96), channel_id=1, source_target_pairs={{0,0},{1,2},{2,8},{3,10},{4,16},{5,18},{6,24},{7,26},{8,4},{9,6},{... | collective-permute-start | bytes 196616 | tf_op jit(solution)/shard_map/ppermute | solution.py:503
  174.9 15.0 %collective-permute-start.20 = (bf16[128,256]{1,0:T(8,128)(2,1)}, bf16[128,256]{1,0:T(8,128)(2,1)}, u32[]{:S(2)}, u32[]{:S(2)}) collective-permute-start(bf16[128,256]{1,0:T(8,128)(2,1)} %get-tuple-element.95), channel_id=1, source_target_pairs={{0,1},{1,3},{2,9},{3,11},{4,17},{5,19},{6,25},{7,27},{8,5},{9,7},{... | collective-permute-start | bytes 196616 | tf_op jit(solution)/shard_map/ppermute | solution.py:503
  (10 other events, 17.5 us)
